TPU v7x, 256 devices: a whole 4x4x8 slice. The times are simulated.
256 devices in a mesh: grav: 8 (over y, z_lo), cross: 32 (over z_hi, x, core).
Axes of the slice: x: 4, y: 4, z: 8 (z_hi: 4, z_lo: 2; z = z_hi * 2 + z_lo), core: 2. Of those that a mesh axis runs over, the one named last changes fastest.
Arguments:
- drift: float32 [3, 64, 262144], P(None, None, ('grav', 'cross')), may hold values from -6 to 6
- warm: float32 [3, 64, 262144], P(None, None, ('grav', 'cross')), may hold values from -6 to 6
- gap: float32 [3, 64, 262144], P(None, None, ('grav', 'cross')), may hold values from -6 to 6
- mobility: bfloat16 [8, 192, 192], replicated, may hold values from -0.3125 to 0.3125
- near_list: int32 [4, 32768], P(None, ('grav', 'cross')), may hold values from 0 to 1023, as said below
- send_slot: int32 [4, 8192], P(None, ('grav', 'cross')), may hold values from 0 to 1023, as said below
- land_slot: int32 [4, 8192], P(None, ('grav', 'cross')), may hold values from 0 to 1023, as said below
- contacts: int32 [3, 524288], P(None, ('grav', 'cross')), may hold values from 0 to 1535, as said below
- live: int32 [256], P(('grav', 'cross')), may hold values from 256 to 2048, as said below
Outputs:
- impulse: float32 [3, 64, 262144], P(None, None, ('grav', 'cross'))
- contact_rate: float32 [3, 64, 262144], P(None, None, ('grav', 'cross'))
Inputs may be any that keep to these rules, and one draw needn't show every extreme that they name: `near_list`: per brick, the 512 slots are distinct and none is a send or landing slot. `send_slot`: per brick, the 128 slots are distinct and none is a landing slot. `land_slot`: per brick, the 128 slots are distinct. `contacts`: row 0 is a slot of the brick's own fibres; row 1 is an extended column, never equal to row 0; row 2 a block kind below 8. Bricks of the lowest gravity layer hold 2048 live contacts; every brick holds at least 256.
All inputs are finite; a program needn't handle non-finite values.
Results may differ from a plain program's by a relative error of at most 0.0032.
Values sent between devices are 32-bit elements; how exact they have to be, the bound alone decides.
No kernel may reach another device: no remote copies, remote signals or barrier semaphores. Data moves between devices by JAX's collectives and lax.ppermute only.
A program may use at most 64 MiB of HBM per device.

v0:
```python
import functools

import jax
import jax.numpy as jnp
from jax import lax
from jax.experimental import pallas as pl
from jax.experimental.pallas import tpu as pltpu
from jax.sharding import PartitionSpec as P

SWEEPS = 3
OMEGA = 0.5
FRICTION = 0.4
LANES = 128
CHUNK = 256
RATE_SIZE = 1024
VMEM_LIMIT = 24 * 1024 * 1024
F32 = jnp.float32
BF16 = jnp.bfloat16


def swap(x, axis, offset):
    count = lax.axis_size(axis)
    pairs = []
    for low in range(offset, count, 2):
        high = (low + 1) % count
        pairs += [(low, high), (high, low)]
    return lax.ppermute(x, axis, pairs)


STEPS = (("cross", 1), ("grav", 0), ("grav", 1), ("cross", 0))
CHIP_FIRST = (3, 0, 1, 2)
CHIP_LAST = (0, 1, 2, 3)


def exchange(sent, order):
    return [swap(sent[step], *STEPS[step]) for step in order]


def odd(axis):
    return lax.rem(lax.axis_index(axis), 2) == 1


def outgoing(faces):
    c, g = odd("cross"), odd("grav")
    return (jnp.where(c, faces[3], faces[2]), jnp.where(g, faces[0], faces[1]),
            jnp.where(g, faces[1], faces[0]), jnp.where(c, faces[2], faces[3]))


def incoming(parts, order):
    parts = [parts[order.index(step)] for step in range(len(order))]
    c, g = odd("cross"), odd("grav")
    place = lax.axis_index("grav")
    below, above = jnp.where(g, parts[1], parts[2]), jnp.where(g, parts[2], parts[1])
    return [jnp.where(place == 0, 0.0, below), jnp.where(place == lax.axis_size("grav") - 1, 0.0, above),
            jnp.where(c, parts[3], parts[0]), jnp.where(c, parts[0], parts[3])]


def split(x, parts):
    out = []
    for _ in range(parts - 1):
        part = x.astype(BF16)
        out.append(part)
        x = x - part.astype(F32)
    out.append(x.astype(BF16))
    return jnp.concatenate(out, axis=0)


def join(y, parts):
    rows = y.shape[0] // parts
    total = y[(parts - 1) * rows:]
    for i in range(parts - 2, -1, -1):
        total = total + y[i * rows:(i + 1) * rows]
    return total


def dot(a, b):
    return jnp.dot(a, b, preferred_element_type=F32)


def iota(shape, dim):
    return lax.broadcasted_iota(jnp.int32, shape, dim)


def narrow(x, shape):
    return jnp.broadcast_to(x, shape).astype(jnp.int16)


def onehot(ids, wanted):
    shape = jnp.broadcast_shapes(ids.shape, wanted.shape)
    one, zero = jnp.ones(shape, BF16), jnp.zeros(shape, BF16)
    return jnp.where(narrow(ids, shape) == narrow(wanted, shape), one, zero)


def signed(ids, first, second):
    shape = jnp.broadcast_shapes(ids.shape, first.shape)
    one, zero = jnp.ones(shape, BF16), jnp.zeros(shape, BF16)
    ids = narrow(ids, shape)
    return jnp.where(ids == narrow(first, shape), one, jnp.where(ids == narrow(second, shape), -one, zero))


def column(row):
    size = row.shape[1]
    eye = iota((size, size), 0) == iota((size, size), 1)
    return jnp.sum(jnp.where(eye, row.astype(F32), 0.0), axis=1, keepdims=True).astype(jnp.int32)


def row_of(table):
    return jnp.concatenate([table[i:i + 1] for i in range(table.shape[0])], axis=1)


def project(trial):
    third = trial.shape[0] // 3
    normal = jnp.maximum(trial[:third], 0.0)
    bound = FRICTION * normal
    first = jnp.minimum(jnp.maximum(trial[third:2 * third], -bound), bound)
    second = jnp.minimum(jnp.maximum(trial[2 * third:], -bound), bound)
    return jnp.concatenate([normal, first, second], axis=0)


def lane_group(rows):
    return iota((rows, LANES), 1) // 32


def send_kernel(drift_hbm, warm_hbm, near_hbm, send_hbm, out0, out1, out2, out3, velocity_out,
                drift, warm, near, send, sems, hot_near, hot_send):
    copies = [pltpu.make_async_copy(source, target, sems.at[i]) for i, (source, target) in enumerate(
        ((near_hbm, near), (send_hbm, send), (warm_hbm, warm), (drift_hbm, drift)))]
    for copy in copies:
        copy.start()
    width, fibres = drift.shape
    quarter = width // 4
    slots = iota((fibres, LANES), 0)
    copies[0].wait()
    for face in range(4):
        hot_near[:, face * LANES:(face + 1) * LANES] = onehot(slots, near[face:face + 1, :])
    copies[1].wait()
    hot_send[...] = onehot(slots, row_of(send[...]))
    copies[2].wait()
    warm_now = warm[...]
    leaving = join(dot(split(warm_now, 3), hot_send[...]), 3)
    copies[3].wait()
    velocity = split(drift[...] + warm_now, 3)
    group = lane_group(quarter)
    blocks = []
    for pair in range(2):
        picked = join(dot(velocity, hot_near[:, pair * 256:pair * 256 + 256]), 3)
        velocity_out[:, pair * 256:pair * 256 + 256] = picked
        for i in range(2):
            face = 2 * pair + i
            packed = jnp.zeros((quarter, LANES), F32)
            for q in range(4):
                rows = leaving[q * quarter:(q + 1) * quarter]
                moved = pltpu.roll(rows, (32 * (q - face)) % LANES, 1) if q != face else rows
                packed = jnp.where(group == q, moved, packed)
            blocks.append((picked[:, i * LANES:(i + 1) * LANES], packed))
    for out, block, packed in zip((out0, out1, out2, out3), outgoing([b[0] for b in blocks]),
                                  outgoing([b[1] for b in blocks])):
        out[:width, :] = block
        out[width:, :] = packed


def setup_kernel(live, drift, warm, gap, near, send, land, contacts, mobility, near_velocity,
                 table, hot_first, hot_near, hot_land, kind, partial, lam, near_state, stacked):
    width, fibres = drift.shape
    count = contacts.shape[1]
    total = table.shape[0]

    land_row = row_of(land[...])
    land_column = column(land_row)

    for start in range(0, count, CHUNK):
        at = slice(start, start + CHUNK)
        alive = start + iota((1, CHUNK), 1) < live[0]
        first = jnp.where(alive, contacts[0:1, at], -1)
        second = jnp.where(alive, contacts[1:2, at], -1)
        for row in range(0, total - LANES, LANES):
            table[row:row + LANES, at] = signed(row + iota((LANES, CHUNK), 0), first, second)
        table[total - LANES:, at] = signed(land_column, first, second)

    for start in range(0, count, LANES):
        at = slice(start, start + LANES)
        first = column(contacts[0:1, at])
        hot_first[at, :] = onehot(first, iota((LANES, fibres), 1))
        for face in range(4):
            hot_near[at, face * LANES:(face + 1) * LANES] = onehot(first, near[face:face + 1, :])

    stacked[...] = jnp.concatenate([mobility[i] for i in range(mobility.shape[0])], axis=1)

    taken = (column(row_of(send[...])) == iota((LANES, fibres), 1)) | (land_column == iota((LANES, fibres), 1))
    keep = jnp.max(jnp.where(taken, 1.0, 0.0), axis=0, keepdims=True) < 0.5
    hot_land[...] = onehot(land_column, iota((LANES, fibres), 1))
    kind[...] = contacts[2:3, :]
    lam_now = jnp.where(keep, warm[...], 0.0)
    lam[...] = lam_now

    slots = iota((fibres, LANES), 0)
    for pair in range(2):
        hot = jnp.concatenate([onehot(slots, near[2 * pair + i:2 * pair + i + 1, :]) for i in range(2)], axis=1)
        at = slice(pair * 256, pair * 256 + 256)
        near_warm = join(dot(split(warm[...], 3), hot), 3)
        near_state[0, :, at] = near_velocity[:, at] - near_warm
        near_state[1, :, at] = join(dot(split(gap[...], 3), hot), 3)
        near_state[2, :, at] = near_warm

    own_part(drift, lam, table, partial)


def own_part(drift, lam, table, partial):
    fibres = drift.shape[1]
    velocity = split(drift[...] + lam[...], 3)

    for start in range(0, partial.shape[1], CHUNK):
        at = slice(start, start + CHUNK)
        partial[:, at] = join(dot(velocity, table[:fibres, at]), 3)


def rate_body(partial, extra, table, base, stacked, kind_row, rate_out):
    width, count = partial.shape
    kinds = stacked.shape[1] // width
    rows = extra.shape[1]
    for start in range(0, count, RATE_SIZE):
        at = slice(start, start + RATE_SIZE)
        far = join(dot(extra[...], table[base:base + rows, at]), 3)
        diff = (partial[:, at] + far).astype(BF16)
        kind = kind_row[:, at]
        none = jnp.zeros_like(diff)
        chosen = jnp.concatenate([jnp.where(kind == i, diff, none) for i in range(kinds)], axis=0)
        rate_out[:, at] = split(dot(stacked[...], chosen), 2)


def near_update(near_in, near_state, near_lam, rate, hot_near, outs):
    faces = []
    for pair in range(2):
        at = slice(pair * 256, pair * 256 + 256)
        rates = join(dot(rate[...], hot_near[:, at]), 2)
        lam = project(near_in[:, at] - OMEGA * (rates + near_state[1, :, at]))
        near_lam[:, at] = lam
        velocity = near_state[0, :, at] + lam
        faces += [velocity[:, i * LANES:(i + 1) * LANES] for i in range(2)]
    for out, block in zip(outs, outgoing(faces)):
        out[...] = block


def first_kernel(part0, part1, part2, part3, hot_land, lam_in, partial, table, stacked, kind,
                 hot_near, near_state, rate, near_lam, lam, out0, out1, out2, out3, extra):
    width, fibres = lam_in.shape
    quarter = width // 4
    parts = (part0, part1, part2, part3)
    blocks = incoming([part[:width, :] for part in parts], CHIP_LAST)
    packed = incoming([part[width:, :] for part in parts], CHIP_LAST)
    group = lane_group(quarter)
    arrived = []
    for q in range(4):
        block = jnp.zeros((quarter, LANES), F32)
        for face in range(4):
            rows = packed[face]
            moved = pltpu.roll(rows, (32 * (face - q)) % LANES, 1) if q != face else rows
            block = jnp.where(group == face, moved, block)
        arrived.append(block)
    arrived = jnp.concatenate(arrived, axis=0)
    near = len(blocks) * LANES
    for i, block in enumerate(blocks + [arrived]):
        extra[:, i * LANES:(i + 1) * LANES] = split(block, 3)
    rate_body(partial, extra, table, fibres, stacked, kind, rate)
    near_update(near_state[2], near_state, near_lam, rate, hot_near, (out0, out1, out2, out3))
    lam[...] = lam_in[...] + join(dot(extra[:, near:], hot_land[...]), 3)


def sweep_kernel(part0, part1, part2, part3, partial, table, stacked, kind,
                 hot_near, near_state, near_in, rate, near_lam, out0, out1, out2, out3, extra):
    parts = [part[...] for part in (part0, part1, part2, part3)]
    for i, block in enumerate(incoming(parts, CHIP_LAST)):
        extra[:, i * LANES:(i + 1) * LANES] = split(block, 3)
    fibres = table.shape[0] - LANES - extra.shape[1]
    rate_body(partial, extra, table, fibres, stacked, kind, rate)
    near_update(near_in, near_state, near_lam, rate, hot_near, (out0, out1, out2, out3))


def update(rate, hot_first, lam_in, gap, lam, at, rates=None):
    total = join(dot(rate[...], hot_first[:, at]), 2)
    lam[:, at] = project(lam_in[:, at] - OMEGA * (total + gap[:, at]))
    if rates is not None:
        rates[:, at] = total


def own_kernel(rate, hot_first, lam_in, gap, drift, table, lam, partial):
    for start in range(0, lam.shape[1], CHUNK):
        update(rate, hot_first, lam_in, gap, lam, slice(start, start + CHUNK))
    own_part(drift, lam, table, partial)


def last_kernel(part0, part1, part2, part3, partial, table, stacked, kind,
                hot_first, lam_in, gap, lam_out, rates_out, rate, extra, lam, rates, sems):
    parts = [part[...] for part in (part0, part1, part2, part3)]
    for i, block in enumerate(incoming(parts, CHIP_FIRST)):
        extra[:, i * LANES:(i + 1) * LANES] = split(block, 3)
    fibres = table.shape[0] - LANES - extra.shape[1]
    rate_body(partial, extra, table, fibres, stacked, kind, rate)
    copies = []
    for n, start in enumerate(range(0, lam.shape[1], CHUNK)):
        at = slice(start, start + CHUNK)
        update(rate, hot_first, lam_in, gap, lam, at, rates)
        for i, (source, target) in enumerate(((lam, lam_out), (rates, rates_out))):
            copy = pltpu.make_async_copy(source.at[:, at], target.at[:, at], sems.at[n, i])
            copy.start()
            copies.append(copy)
    for copy in copies:
        copy.wait()


def call(kernel, outs, args, scalars=0, scratch=(), flops=0, space=pltpu.VMEM, out_space=pltpu.VMEM):
    scalar = pl.BlockSpec(memory_space=pltpu.SMEM)
    return pl.pallas_call(
        kernel,
        out_shape=[jax.ShapeDtypeStruct(s, d) for s, d in outs],
        in_specs=[scalar] * scalars + [pl.BlockSpec(memory_space=space)] * (len(args) - scalars),
        out_specs=[pl.BlockSpec(memory_space=out_space)] * len(outs),
        scratch_shapes=list(scratch),
        compiler_params=pltpu.CompilerParams(vmem_limit_bytes=VMEM_LIMIT),
        cost_estimate=pl.CostEstimate(flops=flops, bytes_accessed=4 << 20, transcendentals=0),
    )(*args)


def per_device(drift, warm, gap, mobility, near_list, send_slot, land_slot, contacts, live):
    width, fibres = drift.shape[0] * drift.shape[1], drift.shape[2]
    count = contacts.shape[1]
    near = near_list.shape[0] * near_list.shape[1]
    shape = drift.shape
    drift, warm, gap = (x.reshape(width, fibres) for x in (drift, warm, gap))
    total = fibres + near + LANES
    face = ((width, LANES), F32)
    big = ((width, fibres), F32)
    rate_shape = ((2 * width, count), BF16)
    near_shape = ((width, near), F32)
    partial_shape = ((width, count), F32)

    held = [pltpu.with_memory_space_constraint(x, pltpu.HBM) for x in (drift, warm, near_list, send_slot)]
    *sent, near_velocity = call(
        send_kernel, [((width + width // 4, LANES), F32)] * 4 + [near_shape], held, flops=2 << 30, space=pltpu.HBM,
        scratch=[pltpu.VMEM(x.shape, x.dtype) for x in held] + [pltpu.SemaphoreType.DMA((len(held),)), pltpu.VMEM((fibres, near), BF16), pltpu.VMEM((fibres, LANES), BF16)])
    halo = exchange(sent, CHIP_LAST)
    table, hot_first, hot_near, hot_land, kind, partial, lam, near_state, stacked = call(
        setup_kernel,
        [((total, count), BF16), ((count, fibres), BF16), ((count, near), BF16), ((LANES, fibres), BF16),
         ((1, count), jnp.int32), partial_shape, big, ((3, width, near), F32),
         ((width, mobility.shape[0] * width), BF16)],
        (live, drift, warm, gap, near_list, send_slot, land_slot, contacts, mobility, near_velocity), scalars=1,
        flops=8 << 30)
    rate, near_lam, lam, *sent = call(
        first_kernel, [rate_shape, near_shape, big] + [face] * 4,
        (*halo, hot_land, lam, partial, table, stacked, kind, hot_near, near_state),
        scratch=[pltpu.VMEM((3 * width, near + LANES), BF16)], flops=4 << 30)
    for repeat in range(1, SWEEPS):
        halo = exchange(sent, CHIP_LAST if repeat < SWEEPS - 1 else CHIP_FIRST)
        lam, partial = call(own_kernel, [big, partial_shape], (rate, hot_first, lam, gap, drift, table),
                            flops=8 << 30)
        extra = pltpu.VMEM((3 * width, near), BF16)
        if repeat < SWEEPS - 1:
            rate, near_lam, *sent = call(
                sweep_kernel, [rate_shape, near_shape] + [face] * 4,
                (*halo, partial, table, stacked, kind, hot_near, near_state, near_lam),
                scratch=[extra], flops=4 << 30)
    lam, rates = call(
        last_kernel, [big, big],
        (*halo, partial, table, stacked, kind, hot_first, lam, gap),
        scratch=[pltpu.VMEM(*rate_shape), extra, pltpu.VMEM(*big), pltpu.VMEM(*big),
                 pltpu.SemaphoreType.DMA((fibres // CHUNK, 2))], flops=4 << 30, out_space=pltpu.HBM)
    return lam.reshape(shape), rates.reshape(shape)


def solution(mesh):
    both = ("grav", "cross")
    return jax.shard_map(
        per_device,
        mesh=mesh,
        in_specs=(
            P(None, None, both),
            P(None, None, both),
            P(None, None, both),
            P(),
            P(None, both),
            P(None, both),
            P(None, both),
            P(None, both),
            P(both),
        ),
        out_specs=(P(None, None, both), P(None, None, both)),
        check_vma=False,
    )
```

profile of v0, /device:TPU:8, one launch (start us, length us, event | category | flops | bytes accessed | tf_op | source)
XLA Modules:
  0.0 55.2 jit_solution(17283571841028136841)
XLA Ops:
  0.7 2.6 %shard_map.104 = (f32[240,128]{1,0:T(8,128)S(1)}, f32[240,128]{1,0:T(8,128)S(1)}, f32[240,128]{1,0:T(8,128)S(1)}, f32[240,128]{1,0:T(8,128)S(1)}, f32[192,512]{1,0:T(8,128)S(1)}) custom-call(f32[192,1024]{1,0:T(8,128)} %bitcast.7, f32[192,1024]{1,0:T(8,128)} %bitcast.5, s32[4,128]{1,0:T(4,128)} %near.1, s32[4,32]{1,0:T(4,128)} %send.1), custom_call_target="tpu_custom_call" | custom-call | flops 2147483648 | bytes 4194304 | tf_op jit(solution)/shard_map/pallas_call | solution.py:313
  3.3 8.0 %collective-permute-start = (f32[240,128]{1,0:T(8,128)S(1)}, f32[240,128]{1,0:T(8,128)S(1)}, u32[]{:S(2)}, u32[]{:S(2)}) collective-permute-start(f32[240,128]{1,0:T(8,128)S(1)} %get-tuple-element.34), channel_id=1, source_target_pairs={{1,2},{2,1},{3,4},{4,3},{5,6},{6,5},{7,8},{8,7},{9,10},{10,9},{11,... | collective-permute-start | bytes 368648 | tf_op jit(solution)/shard_map/ppermute | solution.py:27
  11.3 1.0 %collective-permute-start.1 = (f32[240,128]{1,0:T(8,128)S(1)}, f32[240,128]{1,0:T(8,128)S(1)}, u32[]{:S(2)}, u32[]{:S(2)}) collective-permute-start(f32[240,128]{1,0:T(8,128)S(1)} %get-tuple-element.35), channel_id=1, source_target_pairs={{0,32},{32,0},{64,96},{96,64},{128,160},{160,128},{192,224},{224,1... | collective-permute-start | bytes 368648 | tf_op jit(solution)/shard_map/ppermute | solution.py:27
  12.3 0.9 %collective-permute-start.2 = (f32[240,128]{1,0:T(8,128)S(1)}, f32[240,128]{1,0:T(8,128)S(1)}, u32[]{:S(2)}, u32[]{:S(2)}) collective-permute-start(f32[240,128]{1,0:T(8,128)S(1)} %get-tuple-element.36), channel_id=1, source_target_pairs={{32,64},{64,32},{96,128},{128,96},{160,192},{192,160},{224,0},{0,2... | collective-permute-start | bytes 368648 | tf_op jit(solution)/shard_map/ppermute | solution.py:27
  14.0 5.1 %shard_map.105 = (bf16[1664,2048]{1,0:T(8,128)(2,1)S(1)}, bf16[2048,1024]{1,0:T(8,128)(2,1)S(1)}, bf16[2048,512]{1,0:T(8,128)(2,1)S(1)}, bf16[128,1024]{1,0:T(8,...) custom-call(s32[1]{0:T(128)S(6)} %copy.11.live, ...), custom_call_target="tpu_custom_call" | custom-call | flops 8589934592 | bytes 4194304 | tf_op jit(solution)/shard_map/pallas_call | solution.py:313
  19.1 0.0 collective-permute-done.part0
  19.1 0.0 collective-permute-done.2.part2
  19.1 0.0 collective-permute-done.3.part3
  19.1 4.5 %shard_map.106 = (bf16[384,2048]{1,0:T(8,128)(2,1)S(1)}, f32[192,512]{1,0:T(8,128)S(1)}, f32[192,1024]{1,0:T(8,128)S(1)}, f32[192,128]{1,0:T(8,128)S(1)}, f32[19...) custom-call(f32[240,128]{1,0:T(8,128)S(1)} %collective-permute-done.part0, ...), custom_call_target="tpu_custom_call" | custom-call | flops 4294967296 | bytes 4194304 | tf_op jit(solution)/shard_map/pallas_call | solution.py:313
  23.6 2.2 %collective-permute-start.4 = (f32[192,128]{1,0:T(8,128)S(1)}, f32[192,128]{1,0:T(8,128)S(1)}, u32[]{:S(2)}, u32[]{:S(2)}) collective-permute-start(f32[192,128]{1,0:T(8,128)S(1)} %get-tuple-element.47), channel_id=1, source_target_pairs={{1,2},{2,1},{3,4},{4,3},{5,6},{6,5},{7,8},{8,7},{9,10},{10,9},{11,... | collective-permute-start | bytes 294920 | tf_op jit(solution)/shard_map/ppermute | solution.py:27
  25.9 1.2 %collective-permute-start.5 = (f32[192,128]{1,0:T(8,128)S(1)}, f32[192,128]{1,0:T(8,128)S(1)}, u32[]{:S(2)}, u32[]{:S(2)}) collective-permute-start(f32[192,128]{1,0:T(8,128)S(1)} %get-tuple-element.48), channel_id=1, source_target_pairs={{0,32},{32,0},{64,96},{96,64},{128,160},{160,128},{192,224},{224,1... | collective-permute-start | bytes 294920 | tf_op jit(solution)/shard_map/ppermute | solution.py:27
  27.0 2.1 %collective-permute-start.6 = (f32[192,128]{1,0:T(8,128)S(1)}, f32[192,128]{1,0:T(8,128)S(1)}, u32[]{:S(2)}, u32[]{:S(2)}) collective-permute-start(f32[192,128]{1,0:T(8,128)S(1)} %get-tuple-element.49), channel_id=1, source_target_pairs={{32,64},{64,32},{96,128},{128,96},{160,192},{192,160},{224,0},{0,2... | collective-permute-start | bytes 294920 | tf_op jit(solution)/shard_map/ppermute | solution.py:27
  29.1 0.0 collective-permute-start.7
  29.1 4.5 %shard_map.107 = (f32[192,1024]{1,0:T(8,128)S(1)}, f32[192,2048]{1,0:T(8,128)S(1)}) custom-call(bf16[384,2048]{1,0:T(8,128)(2,1)S(1)} %get-tuple-element.51.rate, bf16[2048,1024]{1,0:T(8,128)(2,1)S(1)} %get-tuple-element.52.hot_first, f32[192,1024]{1,0:T(8,128)S(1)} %get-tuple-element.53.lam_in, f32[192,1024]{1,0:T(8,128)S(1)} %bitcast.12, ...), custom_call_target="tpu_custom_call" | custom-call | flops 8589934592 | bytes 4194304 | tf_op jit(solution)/shard_map/pallas_call | solution.py:313
  33.6 0.3 collective-permute-done.4.part0
  33.8 0.0 collective-permute-done.6.part2
  33.9 4.3 %shard_map.108 = (bf16[384,2048]{1,0:T(8,128)(2,1)S(1)}, f32[192,512]{1,0:T(8,128)}, f32[192,128]{1,0:T(8,128)S(1)}, f32[192,128]{1,0:T(8,128)S(1)}, f32[192,128]{1,0:T(8,128)S(1)}, /*index=5*/f32[192,128]{1,0:T(8,128)S(1)}) custom-call(f32[192,128]{1,0:T(8,128)S(1)} %collective-permute-done.4.part0, f32[192,128]{1,0:T(8,128)S(1)} %collective-permute-done.5.part1, ...), custom_call_target="tpu_custom_call" | custom-call | flops 4294967296 | bytes 4194304 | tf_op jit(solution)/shard_map/pallas_call | solution.py:313
  38.2 0.2 collective-permute-start.8
  38.4 4.5 %collective-permute-start.9 = (f32[192,128]{1,0:T(8,128)S(1)}, f32[192,128]{1,0:T(8,128)S(1)}, u32[]{:S(2)}, u32[]{:S(2)}) collective-permute-start(f32[192,128]{1,0:T(8,128)S(1)} %get-tuple-element.57), channel_id=1, source_target_pairs={{1,2},{2,1},{3,4},{4,3},{5,6},{6,5},{7,8},{8,7},{9,10},{10,9},{11,... | collective-permute-start | bytes 294920 | tf_op jit(solution)/shard_map/ppermute | solution.py:27
  42.9 0.4 collective-permute-start.10
  43.3 1.8 %collective-permute-start.11 = (f32[192,128]{1,0:T(8,128)S(1)}, f32[192,128]{1,0:T(8,128)S(1)}, u32[]{:S(2)}, u32[]{:S(2)}) collective-permute-start(f32[192,128]{1,0:T(8,128)S(1)} %get-tuple-element.59), channel_id=1, source_target_pairs={{32,64},{64,32},{96,128},{128,96},{160,192},{192,160},{224,0},{0,2... | collective-permute-start | bytes 294920 | tf_op jit(solution)/shard_map/ppermute | solution.py:27
  45.1 4.4 %shard_map.109 = (f32[192,1024]{1,0:T(8,128)S(1)}, f32[192,2048]{1,0:T(8,128)S(1)}) custom-call(bf16[384,2048]{1,0:T(8,128)(2,1)S(1)} %get-tuple-element.60.rate, bf16[2048,1024]{1,0:T(8,128)(2,1)S(1)} %get-tuple-element.52.hot_first, f32[192,1024]{1,0:T(8,128)S(1)} %get-tuple-element.61.lam_in, f32[192,1024]{1,0:T(8,128)S(1)} %bitcast.13, ...), custom_call_target="tpu_custom_call" | custom-call | flops 8589934592 | bytes 4194304 | tf_op jit(solution)/shard_map/pallas_call | solution.py:313
  49.6 0.0 collective-permute-done.8.part0
  49.6 5.4 %shard_map.110 = (f32[192,1024]{1,0:T(8,128)}, f32[192,1024]{1,0:T(8,128)}) custom-call(f32[192,128]{1,0:T(8,128)S(1)} %collective-permute-done.8.part0, f32[192,128]{1,0:T(8,128)S(1)} %collective-permute-done.9.part1, f32[192,128]{1,0:T(8,128)S(1)} %collective-permute-done.10.part2, f32[192,128]{1,0:T(8,128)S(1)} %collective-permute-done.11.part3, ...), custom_call_target="tpu_custom_call" | custom-call | flops 4294967296 | bytes 4194304 | tf_op jit(solution)/shard_map/pallas_call | solution.py:313
  (23 shorter events, 0.1 us)
Async XLA Ops:
  0.6 13.3 %copy-start = (f32[3,64,1024]{2,1,0:T(8,128)S(1)}, f32[3,64,1024]{2,1,0:T(8,128)}, u32[]{:S(2)}) copy-start(f32[3,64,1024]{2,1,0:T(8,128)} %param.10) | copy-start | bytes 2359300
  0.6 13.3 %copy-start.1 = (bf16[8,192,192]{2,1,0:T(8,128)(2,1)S(1)}, bf16[8,192,192]{2,1,0:T(8,128)(2,1)}, u32[]{:S(2)}) copy-start(bf16[8,192,192]{2,1,0:T(8,128)(2,1)} %mobility.1) | copy-start | bytes 1769476
  0.7 13.3 %copy-start.2 = (f32[3,64,1024]{2,1,0:T(8,128)S(1)}, f32[3,64,1024]{2,1,0:T(8,128)}, u32[]{:S(2)}) copy-start(f32[3,64,1024]{2,1,0:T(8,128)} %param.9) | copy-start | bytes 2359300
  0.7 13.3 %copy-start.3 = (f32[3,64,1024]{2,1,0:T(8,128)S(1)}, f32[3,64,1024]{2,1,0:T(8,128)}, u32[]{:S(2)}) copy-start(f32[3,64,1024]{2,1,0:T(8,128)} %param.11) | copy-start | bytes 2359300
  0.7 13.3 %copy-start.4 = (s32[3,2048]{1,0:T(4,128)S(1)}, s32[3,2048]{1,0:T(4,128)}, u32[]{:S(2)}) copy-start(s32[3,2048]{1,0:T(4,128)} %contacts.1) | copy-start | bytes 73732
  0.7 13.3 %copy-start.5 = (s32[4,128]{1,0:T(4,128)S(1)}, s32[4,128]{1,0:T(4,128)}, u32[]{:S(2)}) copy-start(s32[4,128]{1,0:T(4,128)} %near.1) | copy-start | bytes 6148
  0.7 13.3 %copy-start.6 = (s32[4,32]{1,0:T(4,128)S(1)}, s32[4,32]{1,0:T(4,128)}, u32[]{:S(2)}) copy-start(s32[4,32]{1,0:T(4,128)} %send.1) | copy-start | bytes 1540
  0.7 13.3 %copy-start.7 = (s32[4,32]{1,0:T(4,128)S(1)}, s32[4,32]{1,0:T(4,128)}, u32[]{:S(2)}) copy-start(s32[4,32]{1,0:T(4,128)} %land.1) | copy-start | bytes 1540
  3.3 15.8 %collective-permute-start = (f32[240,128]{1,0:T(8,128)S(1)}, f32[240,128]{1,0:T(8,128)S(1)}, u32[]{:S(2)}, u32[]{:S(2)}) collective-permute-start(f32[240,128]{1,0:T(8,128)S(1)} %get-tuple-element.34), channel_id=1, source_target_pairs={{1,2},{2,1},{3,4},{4,3},{5,6},{6,5},{7,8},{8,7},{9,10},{10,9},{11,... | collective-permute-start | bytes 368648 | tf_op jit(solution)/shard_map/ppermute | solution.py:27
  11.3 7.8 %collective-permute-start.1 = (f32[240,128]{1,0:T(8,128)S(1)}, f32[240,128]{1,0:T(8,128)S(1)}, u32[]{:S(2)}, u32[]{:S(2)}) collective-permute-start(f32[240,128]{1,0:T(8,128)S(1)} %get-tuple-element.35), channel_id=1, source_target_pairs={{0,32},{32,0},{64,96},{96,64},{128,160},{160,128},{192,224},{224,1... | collective-permute-start | bytes 368648 | tf_op jit(solution)/shard_map/ppermute | solution.py:27
  12.3 6.8 %collective-permute-start.2 = (f32[240,128]{1,0:T(8,128)S(1)}, f32[240,128]{1,0:T(8,128)S(1)}, u32[]{:S(2)}, u32[]{:S(2)}) collective-permute-start(f32[240,128]{1,0:T(8,128)S(1)} %get-tuple-element.36), channel_id=1, source_target_pairs={{32,64},{64,32},{96,128},{128,96},{160,192},{192,160},{224,0},{0,2... | collective-permute-start | bytes 368648 | tf_op jit(solution)/shard_map/ppermute | solution.py:27
  13.2 5.9 %collective-permute-start.3 = (f32[240,128]{1,0:T(8,128)S(1)}, f32[240,128]{1,0:T(8,128)S(1)}, u32[]{:S(2)}, u32[]{:S(2)}) collective-permute-start(f32[240,128]{1,0:T(8,128)S(1)} %get-tuple-element.37), channel_id=1, source_target_pairs={{0,1},{1,0},{2,3},{3,2},{4,5},{5,4},{6,7},{7,6},{8,9},{9,8},{10,11... | collective-permute-start | bytes 368648 | tf_op jit(solution)/shard_map/ppermute | solution.py:27
  23.6 10.2 %collective-permute-start.4 = (f32[192,128]{1,0:T(8,128)S(1)}, f32[192,128]{1,0:T(8,128)S(1)}, u32[]{:S(2)}, u32[]{:S(2)}) collective-permute-start(f32[192,128]{1,0:T(8,128)S(1)} %get-tuple-element.47), channel_id=1, source_target_pairs={{1,2},{2,1},{3,4},{4,3},{5,6},{6,5},{7,8},{8,7},{9,10},{10,9},{11,... | collective-permute-start | bytes 294920 | tf_op jit(solution)/shard_map/ppermute | solution.py:27
  25.9 8.0 %collective-permute-start.5 = (f32[192,128]{1,0:T(8,128)S(1)}, f32[192,128]{1,0:T(8,128)S(1)}, u32[]{:S(2)}, u32[]{:S(2)}) collective-permute-start(f32[192,128]{1,0:T(8,128)S(1)} %get-tuple-element.48), channel_id=1, source_target_pairs={{0,32},{32,0},{64,96},{96,64},{128,160},{160,128},{192,224},{224,1... | collective-permute-start | bytes 294920 | tf_op jit(solution)/shard_map/ppermute | solution.py:27
  27.0 6.9 %collective-permute-start.6 = (f32[192,128]{1,0:T(8,128)S(1)}, f32[192,128]{1,0:T(8,128)S(1)}, u32[]{:S(2)}, u32[]{:S(2)}) collective-permute-start(f32[192,128]{1,0:T(8,128)S(1)} %get-tuple-element.49), channel_id=1, source_target_pairs={{32,64},{64,32},{96,128},{128,96},{160,192},{192,160},{224,0},{0,2... | collective-permute-start | bytes 294920 | tf_op jit(solution)/shard_map/ppermute | solution.py:27
  29.1 4.8 %collective-permute-start.7 = (f32[192,128]{1,0:T(8,128)S(1)}, f32[192,128]{1,0:T(8,128)S(1)}, u32[]{:S(2)}, u32[]{:S(2)}) collective-permute-start(f32[192,128]{1,0:T(8,128)S(1)} %get-tuple-element.50), channel_id=1, source_target_pairs={{0,1},{1,0},{2,3},{3,2},{4,5},{5,4},{6,7},{7,6},{8,9},{9,8},{10,11... | collective-permute-start | bytes 294920 | tf_op jit(solution)/shard_map/ppermute | solution.py:27
  38.2 11.4 %collective-permute-start.8 = (f32[192,128]{1,0:T(8,128)S(1)}, f32[192,128]{1,0:T(8,128)S(1)}, u32[]{:S(2)}, u32[]{:S(2)}) collective-permute-start(f32[192,128]{1,0:T(8,128)S(1)} %get-tuple-element.56), channel_id=1, source_target_pairs={{0,1},{1,0},{2,3},{3,2},{4,5},{5,4},{6,7},{7,6},{8,9},{9,8},{10,11... | collective-permute-start | bytes 294920 | tf_op jit(solution)/shard_map/ppermute | solution.py:27
  38.4 11.2 %collective-permute-start.9 = (f32[192,128]{1,0:T(8,128)S(1)}, f32[192,128]{1,0:T(8,128)S(1)}, u32[]{:S(2)}, u32[]{:S(2)}) collective-permute-start(f32[192,128]{1,0:T(8,128)S(1)} %get-tuple-element.57), channel_id=1, source_target_pairs={{1,2},{2,1},{3,4},{4,3},{5,6},{6,5},{7,8},{8,7},{9,10},{10,9},{11,... | collective-permute-start | bytes 294920 | tf_op jit(solution)/shard_map/ppermute | solution.py:27
  42.9 6.7 %collective-permute-start.10 = (f32[192,128]{1,0:T(8,128)S(1)}, f32[192,128]{1,0:T(8,128)S(1)}, u32[]{:S(2)}, u32[]{:S(2)}) collective-permute-start(f32[192,128]{1,0:T(8,128)S(1)} %get-tuple-element.58), channel_id=1, source_target_pairs={{0,32},{32,0},{64,96},{96,64},{128,160},{160,128},{192,224},{224,1... | collective-permute-start | bytes 294920 | tf_op jit(solution)/shard_map/ppermute | solution.py:27
  43.3 6.3 %collective-permute-start.11 = (f32[192,128]{1,0:T(8,128)S(1)}, f32[192,128]{1,0:T(8,128)S(1)}, u32[]{:S(2)}, u32[]{:S(2)}) collective-permute-start(f32[192,128]{1,0:T(8,128)S(1)} %get-tuple-element.59), channel_id=1, source_target_pairs={{32,64},{64,32},{96,128},{128,96},{160,192},{192,160},{224,0},{0,2... | collective-permute-start | bytes 294920 | tf_op jit(solution)/shard_map/ppermute | solution.py:27
where the time goes:
time: 55.2 us
  Pallas kernels  30.7 us (56%)
  starting transfers between devices  22.3 us (40%)
  between operations  1.7 us (3%)
    pallas_call x7, Pallas kernels, call(): pl.pallas_call(kernel, out_shape=[jax.ShapeDtypeStruct(s, d) for s, d in...  30.7 us
    ppermute x12, starting transfers between devices, swap(): return lax.ppermute(x, axis, pairs)  22.3 us
  transfers between devices with their start and end apart: 12, of which 1 were waited for; matrix products, arithmetic and copies ran while one was open for 0% of the time, Pallas kernels for 25%

commit v1 on v0

--- a/solution.py
+++ b/solution.py
@@ -160,7 +160,7 @@
 
 
 def setup_kernel(live, drift, warm, gap, near, send, land, contacts, mobility, near_velocity,
-                 table, hot_first, hot_near, hot_land, kind, partial, lam, near_state, stacked):
+                 table, hot_near, hot_land, kind, partial, lam, near_state, stacked):
     width, fibres = drift.shape
     count = contacts.shape[1]
     total = table.shape[0]
@@ -180,7 +180,6 @@
     for start in range(0, count, LANES):
         at = slice(start, start + LANES)
         first = column(contacts[0:1, at])
-        hot_first[at, :] = onehot(first, iota((LANES, fibres), 1))
         for face in range(4):
             hot_near[at, face * LANES:(face + 1) * LANES] = onehot(first, near[face:face + 1, :])
 
@@ -241,9 +240,10 @@
         out[...] = block
 
 
-def first_kernel(part0, part1, part2, part3, hot_land, lam_in, partial, table, stacked, kind,
-                 hot_near, near_state, rate, near_lam, lam, out0, out1, out2, out3, extra):
-    width, fibres = lam_in.shape
+def first_kernel(part0, part1, part2, part3, partial, table, stacked, kind,
+                 hot_near, near_state, rate, near_lam, landed, out0, out1, out2, out3, extra):
+    width = partial.shape[0]
+    fibres = table.shape[0] - hot_near.shape[1] - LANES
     quarter = width // 4
     parts = (part0, part1, part2, part3)
     blocks = incoming([part[:width, :] for part in parts], CHIP_LAST)
@@ -263,7 +263,7 @@
         extra[:, i * LANES:(i + 1) * LANES] = split(block, 3)
     rate_body(partial, extra, table, fibres, stacked, kind, rate)
     near_update(near_state[2], near_state, near_lam, rate, hot_near, (out0, out1, out2, out3))
-    lam[...] = lam_in[...] + join(dot(extra[:, near:], hot_land[...]), 3)
+    landed[...] = arrived
 
 
 def sweep_kernel(part0, part1, part2, part3, partial, table, stacked, kind,
@@ -281,6 +281,19 @@
     lam[:, at] = project(lam_in[:, at] - OMEGA * (total + gap[:, at]))
     if rates is not None:
         rates[:, at] = total
+
+
+def own_first_kernel(rate, contacts, landed, hot_land, lam_in, gap, drift, table, lam, partial, hot_first):
+    arrived = split(landed[...], 3)
+    firsts = [column(contacts[0:1, start:start + LANES]) for start in range(0, contacts.shape[1], LANES)]
+    for start in range(0, lam.shape[1], CHUNK):
+        at = slice(start, start + CHUNK)
+        for i, first in enumerate(firsts):
+            hot_first[i * LANES:(i + 1) * LANES, at] = onehot(first, start + iota((LANES, CHUNK), 1))
+        before = lam_in[:, at] + join(dot(arrived, hot_land[:, at]), 3)
+        total = join(dot(rate[...], hot_first[:, at]), 2)
+        lam[:, at] = project(before - OMEGA * (total + gap[:, at]))
+    own_part(drift, lam, table, partial)
 
 
 def own_kernel(rate, hot_first, lam_in, gap, drift, table, lam, partial):
@@ -339,21 +352,26 @@
         send_kernel, [((width + width // 4, LANES), F32)] * 4 + [near_shape], held, flops=2 << 30, space=pltpu.HBM,
         scratch=[pltpu.VMEM(x.shape, x.dtype) for x in held] + [pltpu.SemaphoreType.DMA((len(held),)), pltpu.VMEM((fibres, near), BF16), pltpu.VMEM((fibres, LANES), BF16)])
     halo = exchange(sent, CHIP_LAST)
-    table, hot_first, hot_near, hot_land, kind, partial, lam, near_state, stacked = call(
+    table, hot_near, hot_land, kind, partial, lam, near_state, stacked = call(
         setup_kernel,
-        [((total, count), BF16), ((count, fibres), BF16), ((count, near), BF16), ((LANES, fibres), BF16),
+        [((total, count), BF16), ((count, near), BF16), ((LANES, fibres), BF16),
          ((1, count), jnp.int32), partial_shape, big, ((3, width, near), F32),
          ((width, mobility.shape[0] * width), BF16)],
         (live, drift, warm, gap, near_list, send_slot, land_slot, contacts, mobility, near_velocity), scalars=1,
         flops=8 << 30)
-    rate, near_lam, lam, *sent = call(
-        first_kernel, [rate_shape, near_shape, big] + [face] * 4,
-        (*halo, hot_land, lam, partial, table, stacked, kind, hot_near, near_state),
+    rate, near_lam, landed, *sent = call(
+        first_kernel, [rate_shape, near_shape, face] + [face] * 4,
+        (*halo, partial, table, stacked, kind, hot_near, near_state),
         scratch=[pltpu.VMEM((3 * width, near + LANES), BF16)], flops=4 << 30)
     for repeat in range(1, SWEEPS):
         halo = exchange(sent, CHIP_LAST if repeat < SWEEPS - 1 else CHIP_FIRST)
-        lam, partial = call(own_kernel, [big, partial_shape], (rate, hot_first, lam, gap, drift, table),
-                            flops=8 << 30)
+        if repeat == 1:
+            lam, partial, hot_first = call(
+                own_first_kernel, [big, partial_shape, ((count, fibres), BF16)],
+                (rate, contacts, landed, hot_land, lam, gap, drift, table), flops=8 << 30)
+        else:
+            lam, partial = call(own_kernel, [big, partial_shape], (rate, hot_first, lam, gap, drift, table),
+                                flops=8 << 30)
         extra = pltpu.VMEM((3 * width, near), BF16)
         if repeat < SWEEPS - 1:
             rate, near_lam, *sent = call(

time: 55.2 us -> 54.7 us (level)
  transfers between devices with their start and end apart: 12 -> 12, of which waited for: 1 -> 2; matrix products, arithmetic and copies ran while one was open for 0% -> 0% of each run, Pallas kernels for 25% -> 26%
where the time goes in v1:
time: 54.7 us; the launch traced here: 54.6 us
  Pallas kernels  30.2 us (55%)
  starting transfers between devices  22.4 us (41%)
  between operations  1.7 us (3%)
    pallas_call x7, Pallas kernels, call(): pl.pallas_call(kernel, out_shape=[jax.ShapeDtypeStruct(s, d) for s, d in...  30.2 us
    ppermute x12, starting transfers between devices, swap(): return lax.ppermute(x, axis, pairs)  22.4 us
  transfers between devices with their start and end apart: 12, of which 2 were waited for; matrix products, arithmetic and copies ran while one was open for 0% of the time, Pallas kernels for 26%

profile of v1, /device:TPU:8, one launch (start us, length us, event | category | flops | bytes accessed | tf_op | source)
XLA Modules:
  0.0 54.6 jit_solution(4040729643251984804)
XLA Ops:
  0.7 2.6 %shard_map.104 = (f32[240,128]{1,0:T(8,128)S(1)}, f32[240,128]{1,0:T(8,128)S(1)}, f32[240,128]{1,0:T(8,128)S(1)}, f32[240,128]{1,0:T(8,128)S(1)}, f32[192,512]{1,0:T(8,128)S(1)}) custom-call(f32[192,1024]{1,0:T(8,128)} %bitcast.7, f32[192,1024]{1,0:T(8,128)} %bitcast.5, s32[4,128]{1,0:T(4,128)} %near.1, s32[4,32]{1,0:T(4,128)} %send.1), custom_call_target="tpu_custom_call" | custom-call | flops 2147483648 | bytes 4194304 | tf_op jit(solution)/shard_map/pallas_call | solution.py:326
  3.3 8.0 %collective-permute-start = (f32[240,128]{1,0:T(8,128)S(1)}, f32[240,128]{1,0:T(8,128)S(1)}, u32[]{:S(2)}, u32[]{:S(2)}) collective-permute-start(f32[240,128]{1,0:T(8,128)S(1)} %get-tuple-element.34), channel_id=1, source_target_pairs={{1,2},{2,1},{3,4},{4,3},{5,6},{6,5},{7,8},{8,7},{9,10},{10,9},{11,... | collective-permute-start | bytes 368648 | tf_op jit(solution)/shard_map/ppermute | solution.py:27
  11.3 1.0 %collective-permute-start.1 = (f32[240,128]{1,0:T(8,128)S(1)}, f32[240,128]{1,0:T(8,128)S(1)}, u32[]{:S(2)}, u32[]{:S(2)}) collective-permute-start(f32[240,128]{1,0:T(8,128)S(1)} %get-tuple-element.35), channel_id=1, source_target_pairs={{0,32},{32,0},{64,96},{96,64},{128,160},{160,128},{192,224},{224,1... | collective-permute-start | bytes 368648 | tf_op jit(solution)/shard_map/ppermute | solution.py:27
  12.3 0.9 %collective-permute-start.2 = (f32[240,128]{1,0:T(8,128)S(1)}, f32[240,128]{1,0:T(8,128)S(1)}, u32[]{:S(2)}, u32[]{:S(2)}) collective-permute-start(f32[240,128]{1,0:T(8,128)S(1)} %get-tuple-element.36), channel_id=1, source_target_pairs={{32,64},{64,32},{96,128},{128,96},{160,192},{192,160},{224,0},{0,2... | collective-permute-start | bytes 368648 | tf_op jit(solution)/shard_map/ppermute | solution.py:27
  13.2 0.0 collective-permute-start.3
  14.0 4.7 %shard_map.105 = (bf16[1664,2048]{1,0:T(8,128)(2,1)S(1)}, bf16[2048,512]{1,0:T(8,128)(2,1)S(1)}, bf16[128,1024]{1,0:T(8,128)(2,1)S(1)}, s32[1,2048]{1,0:T(1,128)...) custom-call(s32[1]{0:T(128)S(6)} %copy.11.live, ...), custom_call_target="tpu_custom_call" | custom-call | flops 8589934592 | bytes 4194304 | tf_op jit(solution)/shard_map/pallas_call | solution.py:326
  18.7 0.0 collective-permute-done.2.part2
  18.7 4.1 %shard_map.106 = (bf16[384,2048]{1,0:T(8,128)(2,1)S(1)}, f32[192,512]{1,0:T(8,128)S(1)}, f32[192,128]{1,0:T(8,128)S(1)}, f32[192,128]{1,0:T(8,128)S(1)}, f32[192...) custom-call(f32[240,128]{1,0:T(8,128)S(1)} %collective-permute-done.part0, ...), custom_call_target="tpu_custom_call" | custom-call | flops 4294967296 | bytes 4194304 | tf_op jit(solution)/shard_map/pallas_call | solution.py:326
  22.8 2.6 %collective-permute-start.4 = (f32[192,128]{1,0:T(8,128)S(1)}, f32[192,128]{1,0:T(8,128)S(1)}, u32[]{:S(2)}, u32[]{:S(2)}) collective-permute-start(f32[192,128]{1,0:T(8,128)S(1)} %get-tuple-element.45), channel_id=1, source_target_pairs={{1,2},{2,1},{3,4},{4,3},{5,6},{6,5},{7,8},{8,7},{9,10},{10,9},{11,... | collective-permute-start | bytes 294920 | tf_op jit(solution)/shard_map/ppermute | solution.py:27
  25.5 1.2 %collective-permute-start.5 = (f32[192,128]{1,0:T(8,128)S(1)}, f32[192,128]{1,0:T(8,128)S(1)}, u32[]{:S(2)}, u32[]{:S(2)}) collective-permute-start(f32[192,128]{1,0:T(8,128)S(1)} %get-tuple-element.46), channel_id=1, source_target_pairs={{0,32},{32,0},{64,96},{96,64},{128,160},{160,128},{192,224},{224,1... | collective-permute-start | bytes 294920 | tf_op jit(solution)/shard_map/ppermute | solution.py:27
  26.6 1.7 %collective-permute-start.6 = (f32[192,128]{1,0:T(8,128)S(1)}, f32[192,128]{1,0:T(8,128)S(1)}, u32[]{:S(2)}, u32[]{:S(2)}) collective-permute-start(f32[192,128]{1,0:T(8,128)S(1)} %get-tuple-element.47), channel_id=1, source_target_pairs={{32,64},{64,32},{96,128},{128,96},{160,192},{192,160},{224,0},{0,2... | collective-permute-start | bytes 294920 | tf_op jit(solution)/shard_map/ppermute | solution.py:27
  28.4 0.0 collective-permute-start.7
  28.4 4.8 %shard_map.107 = (f32[192,1024]{1,0:T(8,128)S(1)}, f32[192,2048]{1,0:T(8,128)S(1)}, bf16[2048,1024]{1,0:T(8,128)(2,1)S(1)}) custom-call(bf16[384,2048]{1,0:T(8,128)(2,1)S(1)} %get-tuple-element.49.rate, s32[3,2048]{1,0:T(4,128)S(1)} %copy-done.4, f32[192,128]{1,0:T(8,128)S(1)} %get-tuple-element.50.landed, bf16[128,1024]{1,0:T(8,128)(2,1)S(1)} %get-tuple-element.51.hot_land, ...), custom_call_target="tpu_custom_call" | custom-call | flops 8589934592 | bytes 4194304 | tf_op jit(solution)/shard_map/pallas_call | solution.py:326
  33.2 0.1 collective-permute-done.4.part0
  33.3 0.2 collective-permute-done.6.part2
  33.5 0.0 collective-permute-done.7.part3
  33.5 4.3 %shard_map.108 = (bf16[384,2048]{1,0:T(8,128)(2,1)S(1)}, f32[192,512]{1,0:T(8,128)}, f32[192,128]{1,0:T(8,128)S(1)}, f32[192,128]{1,0:T(8,128)S(1)}, f32[192,128]{1,0:T(8,128)S(1)}, /*index=5*/f32[192,128]{1,0:T(8,128)S(1)}) custom-call(f32[192,128]{1,0:T(8,128)S(1)} %collective-permute-done.4.part0, f32[192,128]{1,0:T(8,128)S(1)} %collective-permute-done.5.part1, ...), custom_call_target="tpu_custom_call" | custom-call | flops 4294967296 | bytes 4194304 | tf_op jit(solution)/shard_map/pallas_call | solution.py:326
  37.8 0.3 collective-permute-start.8
  38.0 4.5 %collective-permute-start.9 = (f32[192,128]{1,0:T(8,128)S(1)}, f32[192,128]{1,0:T(8,128)S(1)}, u32[]{:S(2)}, u32[]{:S(2)}) collective-permute-start(f32[192,128]{1,0:T(8,128)S(1)} %get-tuple-element.56), channel_id=1, source_target_pairs={{1,2},{2,1},{3,4},{4,3},{5,6},{6,5},{7,8},{8,7},{9,10},{10,9},{11,... | collective-permute-start | bytes 294920 | tf_op jit(solution)/shard_map/ppermute | solution.py:27
  42.5 0.4 collective-permute-start.10
  42.9 1.8 %collective-permute-start.11 = (f32[192,128]{1,0:T(8,128)S(1)}, f32[192,128]{1,0:T(8,128)S(1)}, u32[]{:S(2)}, u32[]{:S(2)}) collective-permute-start(f32[192,128]{1,0:T(8,128)S(1)} %get-tuple-element.58), channel_id=1, source_target_pairs={{32,64},{64,32},{96,128},{128,96},{160,192},{192,160},{224,0},{0,2... | collective-permute-start | bytes 294920 | tf_op jit(solution)/shard_map/ppermute | solution.py:27
  44.7 4.4 %shard_map.109 = (f32[192,1024]{1,0:T(8,128)S(1)}, f32[192,2048]{1,0:T(8,128)S(1)}) custom-call(bf16[384,2048]{1,0:T(8,128)(2,1)S(1)} %get-tuple-element.59.rate, bf16[2048,1024]{1,0:T(8,128)(2,1)S(1)} %get-tuple-element.60.hot_first, f32[192,1024]{1,0:T(8,128)S(1)} %get-tuple-element.61.lam_in, f32[192,1024]{1,0:T(8,128)S(1)} %bitcast.13, ...), custom_call_target="tpu_custom_call" | custom-call | flops 8589934592 | bytes 4194304 | tf_op jit(solution)/shard_map/pallas_call | solution.py:326
  49.1 0.0 collective-permute-done.8.part0
  49.2 5.3 %shard_map.110 = (f32[192,1024]{1,0:T(8,128)}, f32[192,1024]{1,0:T(8,128)}) custom-call(f32[192,128]{1,0:T(8,128)S(1)} %collective-permute-done.8.part0, f32[192,128]{1,0:T(8,128)S(1)} %collective-permute-done.9.part1, f32[192,128]{1,0:T(8,128)S(1)} %collective-permute-done.10.part2, f32[192,128]{1,0:T(8,128)S(1)} %collective-permute-done.11.part3, ...), custom_call_target="tpu_custom_call" | custom-call | flops 4294967296 | bytes 4194304 | tf_op jit(solution)/shard_map/pallas_call | solution.py:326
  (23 shorter events, 0.1 us)
Async XLA Ops:
  0.6 13.3 %copy-start = (f32[3,64,1024]{2,1,0:T(8,128)S(1)}, f32[3,64,1024]{2,1,0:T(8,128)}, u32[]{:S(2)}) copy-start(f32[3,64,1024]{2,1,0:T(8,128)} %param.10) | copy-start | bytes 2359300
  0.6 13.3 %copy-start.1 = (bf16[8,192,192]{2,1,0:T(8,128)(2,1)S(1)}, bf16[8,192,192]{2,1,0:T(8,128)(2,1)}, u32[]{:S(2)}) copy-start(bf16[8,192,192]{2,1,0:T(8,128)(2,1)} %mobility.1) | copy-start | bytes 1769476
  0.7 13.3 %copy-start.2 = (f32[3,64,1024]{2,1,0:T(8,128)S(1)}, f32[3,64,1024]{2,1,0:T(8,128)}, u32[]{:S(2)}) copy-start(f32[3,64,1024]{2,1,0:T(8,128)} %param.9) | copy-start | bytes 2359300
  0.7 13.3 %copy-start.3 = (f32[3,64,1024]{2,1,0:T(8,128)S(1)}, f32[3,64,1024]{2,1,0:T(8,128)}, u32[]{:S(2)}) copy-start(f32[3,64,1024]{2,1,0:T(8,128)} %param.11) | copy-start | bytes 2359300
  0.7 13.3 %copy-start.4 = (s32[3,2048]{1,0:T(4,128)S(1)}, s32[3,2048]{1,0:T(4,128)}, u32[]{:S(2)}) copy-start(s32[3,2048]{1,0:T(4,128)} %contacts.3) | copy-start | bytes 73732
  0.7 13.3 %copy-start.5 = (s32[4,128]{1,0:T(4,128)S(1)}, s32[4,128]{1,0:T(4,128)}, u32[]{:S(2)}) copy-start(s32[4,128]{1,0:T(4,128)} %near.1) | copy-start | bytes 6148
  0.7 13.3 %copy-start.6 = (s32[4,32]{1,0:T(4,128)S(1)}, s32[4,32]{1,0:T(4,128)}, u32[]{:S(2)}) copy-start(s32[4,32]{1,0:T(4,128)} %send.1) | copy-start | bytes 1540
  0.7 13.3 %copy-start.7 = (s32[4,32]{1,0:T(4,128)S(1)}, s32[4,32]{1,0:T(4,128)}, u32[]{:S(2)}) copy-start(s32[4,32]{1,0:T(4,128)} %land.1) | copy-start | bytes 1540
  3.3 15.4 %collective-permute-start = (f32[240,128]{1,0:T(8,128)S(1)}, f32[240,128]{1,0:T(8,128)S(1)}, u32[]{:S(2)}, u32[]{:S(2)}) collective-permute-start(f32[240,128]{1,0:T(8,128)S(1)} %get-tuple-element.34), channel_id=1, source_target_pairs={{1,2},{2,1},{3,4},{4,3},{5,6},{6,5},{7,8},{8,7},{9,10},{10,9},{11,... | collective-permute-start | bytes 368648 | tf_op jit(solution)/shard_map/ppermute | solution.py:27
  11.3 7.4 %collective-permute-start.1 = (f32[240,128]{1,0:T(8,128)S(1)}, f32[240,128]{1,0:T(8,128)S(1)}, u32[]{:S(2)}, u32[]{:S(2)}) collective-permute-start(f32[240,128]{1,0:T(8,128)S(1)} %get-tuple-element.35), channel_id=1, source_target_pairs={{0,32},{32,0},{64,96},{96,64},{128,160},{160,128},{192,224},{224,1... | collective-permute-start | bytes 368648 | tf_op jit(solution)/shard_map/ppermute | solution.py:27
  12.3 6.4 %collective-permute-start.2 = (f32[240,128]{1,0:T(8,128)S(1)}, f32[240,128]{1,0:T(8,128)S(1)}, u32[]{:S(2)}, u32[]{:S(2)}) collective-permute-start(f32[240,128]{1,0:T(8,128)S(1)} %get-tuple-element.36), channel_id=1, source_target_pairs={{32,64},{64,32},{96,128},{128,96},{160,192},{192,160},{224,0},{0,2... | collective-permute-start | bytes 368648 | tf_op jit(solution)/shard_map/ppermute | solution.py:27
  13.2 5.5 %collective-permute-start.3 = (f32[240,128]{1,0:T(8,128)S(1)}, f32[240,128]{1,0:T(8,128)S(1)}, u32[]{:S(2)}, u32[]{:S(2)}) collective-permute-start(f32[240,128]{1,0:T(8,128)S(1)} %get-tuple-element.37), channel_id=1, source_target_pairs={{0,1},{1,0},{2,3},{3,2},{4,5},{5,4},{6,7},{7,6},{8,9},{9,8},{10,11... | collective-permute-start | bytes 368648 | tf_op jit(solution)/shard_map/ppermute | solution.py:27
  22.8 10.4 %collective-permute-start.4 = (f32[192,128]{1,0:T(8,128)S(1)}, f32[192,128]{1,0:T(8,128)S(1)}, u32[]{:S(2)}, u32[]{:S(2)}) collective-permute-start(f32[192,128]{1,0:T(8,128)S(1)} %get-tuple-element.45), channel_id=1, source_target_pairs={{1,2},{2,1},{3,4},{4,3},{5,6},{6,5},{7,8},{8,7},{9,10},{10,9},{11,... | collective-permute-start | bytes 294920 | tf_op jit(solution)/shard_map/ppermute | solution.py:27
  25.5 7.8 %collective-permute-start.5 = (f32[192,128]{1,0:T(8,128)S(1)}, f32[192,128]{1,0:T(8,128)S(1)}, u32[]{:S(2)}, u32[]{:S(2)}) collective-permute-start(f32[192,128]{1,0:T(8,128)S(1)} %get-tuple-element.46), channel_id=1, source_target_pairs={{0,32},{32,0},{64,96},{96,64},{128,160},{160,128},{192,224},{224,1... | collective-permute-start | bytes 294920 | tf_op jit(solution)/shard_map/ppermute | solution.py:27
  26.6 6.9 %collective-permute-start.6 = (f32[192,128]{1,0:T(8,128)S(1)}, f32[192,128]{1,0:T(8,128)S(1)}, u32[]{:S(2)}, u32[]{:S(2)}) collective-permute-start(f32[192,128]{1,0:T(8,128)S(1)} %get-tuple-element.47), channel_id=1, source_target_pairs={{32,64},{64,32},{96,128},{128,96},{160,192},{192,160},{224,0},{0,2... | collective-permute-start | bytes 294920 | tf_op jit(solution)/shard_map/ppermute | solution.py:27
  28.4 5.2 %collective-permute-start.7 = (f32[192,128]{1,0:T(8,128)S(1)}, f32[192,128]{1,0:T(8,128)S(1)}, u32[]{:S(2)}, u32[]{:S(2)}) collective-permute-start(f32[192,128]{1,0:T(8,128)S(1)} %get-tuple-element.48), channel_id=1, source_target_pairs={{0,1},{1,0},{2,3},{3,2},{4,5},{5,4},{6,7},{7,6},{8,9},{9,8},{10,11... | collective-permute-start | bytes 294920 | tf_op jit(solution)/shard_map/ppermute | solution.py:27
  37.8 11.4 %collective-permute-start.8 = (f32[192,128]{1,0:T(8,128)S(1)}, f32[192,128]{1,0:T(8,128)S(1)}, u32[]{:S(2)}, u32[]{:S(2)}) collective-permute-start(f32[192,128]{1,0:T(8,128)S(1)} %get-tuple-element.55), channel_id=1, source_target_pairs={{0,1},{1,0},{2,3},{3,2},{4,5},{5,4},{6,7},{7,6},{8,9},{9,8},{10,11... | collective-permute-start | bytes 294920 | tf_op jit(solution)/shard_map/ppermute | solution.py:27
  38.0 11.1 %collective-permute-start.9 = (f32[192,128]{1,0:T(8,128)S(1)}, f32[192,128]{1,0:T(8,128)S(1)}, u32[]{:S(2)}, u32[]{:S(2)}) collective-permute-start(f32[192,128]{1,0:T(8,128)S(1)} %get-tuple-element.56), channel_id=1, source_target_pairs={{1,2},{2,1},{3,4},{4,3},{5,6},{6,5},{7,8},{8,7},{9,10},{10,9},{11,... | collective-permute-start | bytes 294920 | tf_op jit(solution)/shard_map/ppermute | solution.py:27
  42.5 6.6 %collective-permute-start.10 = (f32[192,128]{1,0:T(8,128)S(1)}, f32[192,128]{1,0:T(8,128)S(1)}, u32[]{:S(2)}, u32[]{:S(2)}) collective-permute-start(f32[192,128]{1,0:T(8,128)S(1)} %get-tuple-element.57), channel_id=1, source_target_pairs={{0,32},{32,0},{64,96},{96,64},{128,160},{160,128},{192,224},{224,1... | collective-permute-start | bytes 294920 | tf_op jit(solution)/shard_map/ppermute | solution.py:27
  42.9 6.2 %collective-permute-start.11 = (f32[192,128]{1,0:T(8,128)S(1)}, f32[192,128]{1,0:T(8,128)S(1)}, u32[]{:S(2)}, u32[]{:S(2)}) collective-permute-start(f32[192,128]{1,0:T(8,128)S(1)} %get-tuple-element.58), channel_id=1, source_target_pairs={{32,64},{64,32},{96,128},{128,96},{160,192},{192,160},{224,0},{0,2... | collective-permute-start | bytes 294920 | tf_op jit(solution)/shard_map/ppermute | solution.py:27

commit v2 on v1

--- a/solution.py
+++ b/solution.py
@@ -28,8 +28,8 @@
 
 
 STEPS = (("cross", 1), ("grav", 0), ("grav", 1), ("cross", 0))
-CHIP_FIRST = (3, 0, 1, 2)
-CHIP_LAST = (0, 1, 2, 3)
+CHIP_FIRST = (3, 0, 2, 1)
+CHIP_LAST = (0, 2, 1, 3)
 
 
 def exchange(sent, order):

time: 54.7 us -> 54.1 us (0.989)
  starting transfers between devices: 22.4 us -> 21.2 us
    ppermute x12, starting transfers between devices: 22.4 us -> 21.2 us  [swap(): return lax.ppermute(x, axis, pairs)]
where the time goes in v2:
time: 54.1 us; the launch traced here: 54 us
  Pallas kernels  30.2 us (56%)
  starting transfers between devices  21.2 us (39%)
  between operations  1.68 us (3%)
  waiting for transfers between devices  0.85 us (2%)
    pallas_call x7, Pallas kernels, call(): pl.pallas_call(kernel, out_shape=[jax.ShapeDtypeStruct(s, d) for s, d in...  30.2 us
    ppermute x12, starting transfers between devices, swap(): return lax.ppermute(x, axis, pairs)  21.2 us
  transfers between devices with their start and end apart: 12, of which 2 were waited for; matrix products, arithmetic and copies ran while one was open for 0% of the time, Pallas kernels for 26%

profile of v2, /device:TPU:8, one launch (start us, length us, event | category | flops | bytes accessed | tf_op | source)
XLA Modules:
  0.0 54.0 jit_solution(5900331719889276949)
XLA Ops:
  0.7 2.6 %shard_map.104 = (f32[240,128]{1,0:T(8,128)S(1)}, f32[240,128]{1,0:T(8,128)S(1)}, f32[240,128]{1,0:T(8,128)S(1)}, f32[240,128]{1,0:T(8,128)S(1)}, f32[192,512]{1,0:T(8,128)S(1)}) custom-call(f32[192,1024]{1,0:T(8,128)} %bitcast.7, f32[192,1024]{1,0:T(8,128)} %bitcast.5, s32[4,128]{1,0:T(4,128)} %near.1, s32[4,32]{1,0:T(4,128)} %send.1), custom_call_target="tpu_custom_call" | custom-call | flops 2147483648 | bytes 4194304 | tf_op jit(solution)/shard_map/pallas_call | solution.py:326
  3.3 8.0 %collective-permute-start = (f32[240,128]{1,0:T(8,128)S(1)}, f32[240,128]{1,0:T(8,128)S(1)}, u32[]{:S(2)}, u32[]{:S(2)}) collective-permute-start(f32[240,128]{1,0:T(8,128)S(1)} %get-tuple-element.34), channel_id=1, source_target_pairs={{1,2},{2,1},{3,4},{4,3},{5,6},{6,5},{7,8},{8,7},{9,10},{10,9},{11,... | collective-permute-start | bytes 368648 | tf_op jit(solution)/shard_map/ppermute | solution.py:27
  11.3 0.9 %collective-permute-start.1 = (f32[240,128]{1,0:T(8,128)S(1)}, f32[240,128]{1,0:T(8,128)S(1)}, u32[]{:S(2)}, u32[]{:S(2)}) collective-permute-start(f32[240,128]{1,0:T(8,128)S(1)} %get-tuple-element.35), channel_id=1, source_target_pairs={{32,64},{64,32},{96,128},{128,96},{160,192},{192,160},{224,0},{0,2... | collective-permute-start | bytes 368648 | tf_op jit(solution)/shard_map/ppermute | solution.py:27
  12.2 2.1 %collective-permute-start.2 = (f32[240,128]{1,0:T(8,128)S(1)}, f32[240,128]{1,0:T(8,128)S(1)}, u32[]{:S(2)}, u32[]{:S(2)}) collective-permute-start(f32[240,128]{1,0:T(8,128)S(1)} %get-tuple-element.36), channel_id=1, source_target_pairs={{0,32},{32,0},{64,96},{96,64},{128,160},{160,128},{192,224},{224,1... | collective-permute-start | bytes 368648 | tf_op jit(solution)/shard_map/ppermute | solution.py:27
  14.4 0.0 collective-permute-start.3
  15.1 4.7 %shard_map.105 = (bf16[1664,2048]{1,0:T(8,128)(2,1)S(1)}, bf16[2048,512]{1,0:T(8,128)(2,1)S(1)}, bf16[128,1024]{1,0:T(8,128)(2,1)S(1)}, s32[1,2048]{1,0:T(1,128)...) custom-call(s32[1]{0:T(128)S(6)} %copy.11.live, ...), custom_call_target="tpu_custom_call" | custom-call | flops 8589934592 | bytes 4194304 | tf_op jit(solution)/shard_map/pallas_call | solution.py:326
  19.8 0.0 collective-permute-done.1.part1
  19.8 0.0 collective-permute-done.2.part2
  19.9 4.1 %shard_map.106 = (bf16[384,2048]{1,0:T(8,128)(2,1)S(1)}, f32[192,512]{1,0:T(8,128)S(1)}, f32[192,128]{1,0:T(8,128)S(1)}, f32[192,128]{1,0:T(8,128)S(1)}, f32[192...) custom-call(f32[240,128]{1,0:T(8,128)S(1)} %collective-permute-done.part0, ...), custom_call_target="tpu_custom_call" | custom-call | flops 4294967296 | bytes 4194304 | tf_op jit(solution)/shard_map/pallas_call | solution.py:326
  24.0 1.5 %collective-permute-start.4 = (f32[192,128]{1,0:T(8,128)S(1)}, f32[192,128]{1,0:T(8,128)S(1)}, u32[]{:S(2)}, u32[]{:S(2)}) collective-permute-start(f32[192,128]{1,0:T(8,128)S(1)} %get-tuple-element.45), channel_id=1, source_target_pairs={{1,2},{2,1},{3,4},{4,3},{5,6},{6,5},{7,8},{8,7},{9,10},{10,9},{11,... | collective-permute-start | bytes 294920 | tf_op jit(solution)/shard_map/ppermute | solution.py:27
  25.5 1.9 %collective-permute-start.5 = (f32[192,128]{1,0:T(8,128)S(1)}, f32[192,128]{1,0:T(8,128)S(1)}, u32[]{:S(2)}, u32[]{:S(2)}) collective-permute-start(f32[192,128]{1,0:T(8,128)S(1)} %get-tuple-element.46), channel_id=1, source_target_pairs={{32,64},{64,32},{96,128},{128,96},{160,192},{192,160},{224,0},{0,2... | collective-permute-start | bytes 294920 | tf_op jit(solution)/shard_map/ppermute | solution.py:27
  27.3 1.2 %collective-permute-start.6 = (f32[192,128]{1,0:T(8,128)S(1)}, f32[192,128]{1,0:T(8,128)S(1)}, u32[]{:S(2)}, u32[]{:S(2)}) collective-permute-start(f32[192,128]{1,0:T(8,128)S(1)} %get-tuple-element.47), channel_id=1, source_target_pairs={{0,32},{32,0},{64,96},{96,64},{128,160},{160,128},{192,224},{224,1... | collective-permute-start | bytes 294920 | tf_op jit(solution)/shard_map/ppermute | solution.py:27
  28.5 0.0 collective-permute-start.7
  28.5 4.9 %shard_map.107 = (f32[192,1024]{1,0:T(8,128)S(1)}, f32[192,2048]{1,0:T(8,128)S(1)}, bf16[2048,1024]{1,0:T(8,128)(2,1)S(1)}) custom-call(bf16[384,2048]{1,0:T(8,128)(2,1)S(1)} %get-tuple-element.49.rate, s32[3,2048]{1,0:T(4,128)S(1)} %copy-done.4, f32[192,128]{1,0:T(8,128)S(1)} %get-tuple-element.50.landed, bf16[128,1024]{1,0:T(8,128)(2,1)S(1)} %get-tuple-element.51.hot_land, ...), custom_call_target="tpu_custom_call" | custom-call | flops 8589934592 | bytes 4194304 | tf_op jit(solution)/shard_map/pallas_call | solution.py:326
  33.4 0.4 collective-permute-done.4.part0
  33.8 0.0 collective-permute-done.5.part1
  33.8 4.3 %shard_map.108 = (bf16[384,2048]{1,0:T(8,128)(2,1)S(1)}, f32[192,512]{1,0:T(8,128)}, f32[192,128]{1,0:T(8,128)S(1)}, f32[192,128]{1,0:T(8,128)S(1)}, f32[192,128]{1,0:T(8,128)S(1)}, /*index=5*/f32[192,128]{1,0:T(8,128)S(1)}) custom-call(f32[192,128]{1,0:T(8,128)S(1)} %collective-permute-done.4.part0, f32[192,128]{1,0:T(8,128)S(1)} %collective-permute-done.5.part1, ...), custom_call_target="tpu_custom_call" | custom-call | flops 4294967296 | bytes 4194304 | tf_op jit(solution)/shard_map/pallas_call | solution.py:326
  38.1 0.1 collective-permute-start.8
  38.2 3.7 %collective-permute-start.9 = (f32[192,128]{1,0:T(8,128)S(1)}, f32[192,128]{1,0:T(8,128)S(1)}, u32[]{:S(2)}, u32[]{:S(2)}) collective-permute-start(f32[192,128]{1,0:T(8,128)S(1)} %get-tuple-element.56), channel_id=1, source_target_pairs={{1,2},{2,1},{3,4},{4,3},{5,6},{6,5},{7,8},{8,7},{9,10},{10,9},{11,... | collective-permute-start | bytes 294920 | tf_op jit(solution)/shard_map/ppermute | solution.py:27
  41.9 1.8 %collective-permute-start.10 = (f32[192,128]{1,0:T(8,128)S(1)}, f32[192,128]{1,0:T(8,128)S(1)}, u32[]{:S(2)}, u32[]{:S(2)}) collective-permute-start(f32[192,128]{1,0:T(8,128)S(1)} %get-tuple-element.57), channel_id=1, source_target_pairs={{32,64},{64,32},{96,128},{128,96},{160,192},{192,160},{224,0},{0,2... | collective-permute-start | bytes 294920 | tf_op jit(solution)/shard_map/ppermute | solution.py:27
  43.7 0.0 collective-permute-start.11
  43.7 4.4 %shard_map.109 = (f32[192,1024]{1,0:T(8,128)S(1)}, f32[192,2048]{1,0:T(8,128)S(1)}) custom-call(bf16[384,2048]{1,0:T(8,128)(2,1)S(1)} %get-tuple-element.59.rate, bf16[2048,1024]{1,0:T(8,128)(2,1)S(1)} %get-tuple-element.60.hot_first, f32[192,1024]{1,0:T(8,128)S(1)} %get-tuple-element.61.lam_in, f32[192,1024]{1,0:T(8,128)S(1)} %bitcast.13, ...), custom_call_target="tpu_custom_call" | custom-call | flops 8589934592 | bytes 4194304 | tf_op jit(solution)/shard_map/pallas_call | solution.py:326
  48.1 0.4 collective-permute-done.9.part1
  48.6 5.3 %shard_map.110 = (f32[192,1024]{1,0:T(8,128)}, f32[192,1024]{1,0:T(8,128)}) custom-call(f32[192,128]{1,0:T(8,128)S(1)} %collective-permute-done.8.part0, f32[192,128]{1,0:T(8,128)S(1)} %collective-permute-done.9.part1, f32[192,128]{1,0:T(8,128)S(1)} %collective-permute-done.10.part2, f32[192,128]{1,0:T(8,128)S(1)} %collective-permute-done.11.part3, ...), custom_call_target="tpu_custom_call" | custom-call | flops 4294967296 | bytes 4194304 | tf_op jit(solution)/shard_map/pallas_call | solution.py:326
  (23 shorter events, 0.1 us)
Async XLA Ops:
  0.6 14.4 %copy-start = (f32[3,64,1024]{2,1,0:T(8,128)S(1)}, f32[3,64,1024]{2,1,0:T(8,128)}, u32[]{:S(2)}) copy-start(f32[3,64,1024]{2,1,0:T(8,128)} %param.10) | copy-start | bytes 2359300
  0.6 14.4 %copy-start.1 = (bf16[8,192,192]{2,1,0:T(8,128)(2,1)S(1)}, bf16[8,192,192]{2,1,0:T(8,128)(2,1)}, u32[]{:S(2)}) copy-start(bf16[8,192,192]{2,1,0:T(8,128)(2,1)} %mobility.1) | copy-start | bytes 1769476
  0.7 14.4 %copy-start.2 = (f32[3,64,1024]{2,1,0:T(8,128)S(1)}, f32[3,64,1024]{2,1,0:T(8,128)}, u32[]{:S(2)}) copy-start(f32[3,64,1024]{2,1,0:T(8,128)} %param.9) | copy-start | bytes 2359300
  0.7 14.4 %copy-start.3 = (f32[3,64,1024]{2,1,0:T(8,128)S(1)}, f32[3,64,1024]{2,1,0:T(8,128)}, u32[]{:S(2)}) copy-start(f32[3,64,1024]{2,1,0:T(8,128)} %param.11) | copy-start | bytes 2359300
  0.7 14.4 %copy-start.4 = (s32[3,2048]{1,0:T(4,128)S(1)}, s32[3,2048]{1,0:T(4,128)}, u32[]{:S(2)}) copy-start(s32[3,2048]{1,0:T(4,128)} %contacts.3) | copy-start | bytes 73732
  0.7 14.4 %copy-start.5 = (s32[4,128]{1,0:T(4,128)S(1)}, s32[4,128]{1,0:T(4,128)}, u32[]{:S(2)}) copy-start(s32[4,128]{1,0:T(4,128)} %near.1) | copy-start | bytes 6148
  0.7 14.4 %copy-start.6 = (s32[4,32]{1,0:T(4,128)S(1)}, s32[4,32]{1,0:T(4,128)}, u32[]{:S(2)}) copy-start(s32[4,32]{1,0:T(4,128)} %send.1) | copy-start | bytes 1540
  0.7 14.4 %copy-start.7 = (s32[4,32]{1,0:T(4,128)S(1)}, s32[4,32]{1,0:T(4,128)}, u32[]{:S(2)}) copy-start(s32[4,32]{1,0:T(4,128)} %land.1) | copy-start | bytes 1540
  3.3 16.5 %collective-permute-start = (f32[240,128]{1,0:T(8,128)S(1)}, f32[240,128]{1,0:T(8,128)S(1)}, u32[]{:S(2)}, u32[]{:S(2)}) collective-permute-start(f32[240,128]{1,0:T(8,128)S(1)} %get-tuple-element.34), channel_id=1, source_target_pairs={{1,2},{2,1},{3,4},{4,3},{5,6},{6,5},{7,8},{8,7},{9,10},{10,9},{11,... | collective-permute-start | bytes 368648 | tf_op jit(solution)/shard_map/ppermute | solution.py:27
  11.3 8.5 %collective-permute-start.1 = (f32[240,128]{1,0:T(8,128)S(1)}, f32[240,128]{1,0:T(8,128)S(1)}, u32[]{:S(2)}, u32[]{:S(2)}) collective-permute-start(f32[240,128]{1,0:T(8,128)S(1)} %get-tuple-element.35), channel_id=1, source_target_pairs={{32,64},{64,32},{96,128},{128,96},{160,192},{192,160},{224,0},{0,2... | collective-permute-start | bytes 368648 | tf_op jit(solution)/shard_map/ppermute | solution.py:27
  12.2 7.6 %collective-permute-start.2 = (f32[240,128]{1,0:T(8,128)S(1)}, f32[240,128]{1,0:T(8,128)S(1)}, u32[]{:S(2)}, u32[]{:S(2)}) collective-permute-start(f32[240,128]{1,0:T(8,128)S(1)} %get-tuple-element.36), channel_id=1, source_target_pairs={{0,32},{32,0},{64,96},{96,64},{128,160},{160,128},{192,224},{224,1... | collective-permute-start | bytes 368648 | tf_op jit(solution)/shard_map/ppermute | solution.py:27
  14.4 5.5 %collective-permute-start.3 = (f32[240,128]{1,0:T(8,128)S(1)}, f32[240,128]{1,0:T(8,128)S(1)}, u32[]{:S(2)}, u32[]{:S(2)}) collective-permute-start(f32[240,128]{1,0:T(8,128)S(1)} %get-tuple-element.37), channel_id=1, source_target_pairs={{0,1},{1,0},{2,3},{3,2},{4,5},{5,4},{6,7},{7,6},{8,9},{9,8},{10,11... | collective-permute-start | bytes 368648 | tf_op jit(solution)/shard_map/ppermute | solution.py:27
  24.0 9.8 %collective-permute-start.4 = (f32[192,128]{1,0:T(8,128)S(1)}, f32[192,128]{1,0:T(8,128)S(1)}, u32[]{:S(2)}, u32[]{:S(2)}) collective-permute-start(f32[192,128]{1,0:T(8,128)S(1)} %get-tuple-element.45), channel_id=1, source_target_pairs={{1,2},{2,1},{3,4},{4,3},{5,6},{6,5},{7,8},{8,7},{9,10},{10,9},{11,... | collective-permute-start | bytes 294920 | tf_op jit(solution)/shard_map/ppermute | solution.py:27
  25.5 8.3 %collective-permute-start.5 = (f32[192,128]{1,0:T(8,128)S(1)}, f32[192,128]{1,0:T(8,128)S(1)}, u32[]{:S(2)}, u32[]{:S(2)}) collective-permute-start(f32[192,128]{1,0:T(8,128)S(1)} %get-tuple-element.46), channel_id=1, source_target_pairs={{32,64},{64,32},{96,128},{128,96},{160,192},{192,160},{224,0},{0,2... | collective-permute-start | bytes 294920 | tf_op jit(solution)/shard_map/ppermute | solution.py:27
  27.3 6.4 %collective-permute-start.6 = (f32[192,128]{1,0:T(8,128)S(1)}, f32[192,128]{1,0:T(8,128)S(1)}, u32[]{:S(2)}, u32[]{:S(2)}) collective-permute-start(f32[192,128]{1,0:T(8,128)S(1)} %get-tuple-element.47), channel_id=1, source_target_pairs={{0,32},{32,0},{64,96},{96,64},{128,160},{160,128},{192,224},{224,1... | collective-permute-start | bytes 294920 | tf_op jit(solution)/shard_map/ppermute | solution.py:27
  28.5 5.3 %collective-permute-start.7 = (f32[192,128]{1,0:T(8,128)S(1)}, f32[192,128]{1,0:T(8,128)S(1)}, u32[]{:S(2)}, u32[]{:S(2)}) collective-permute-start(f32[192,128]{1,0:T(8,128)S(1)} %get-tuple-element.48), channel_id=1, source_target_pairs={{0,1},{1,0},{2,3},{3,2},{4,5},{5,4},{6,7},{7,6},{8,9},{9,8},{10,11... | collective-permute-start | bytes 294920 | tf_op jit(solution)/shard_map/ppermute | solution.py:27
  38.1 10.1 %collective-permute-start.8 = (f32[192,128]{1,0:T(8,128)S(1)}, f32[192,128]{1,0:T(8,128)S(1)}, u32[]{:S(2)}, u32[]{:S(2)}) collective-permute-start(f32[192,128]{1,0:T(8,128)S(1)} %get-tuple-element.55), channel_id=1, source_target_pairs={{0,1},{1,0},{2,3},{3,2},{4,5},{5,4},{6,7},{7,6},{8,9},{9,8},{10,11... | collective-permute-start | bytes 294920 | tf_op jit(solution)/shard_map/ppermute | solution.py:27
  38.2 10.4 %collective-permute-start.9 = (f32[192,128]{1,0:T(8,128)S(1)}, f32[192,128]{1,0:T(8,128)S(1)}, u32[]{:S(2)}, u32[]{:S(2)}) collective-permute-start(f32[192,128]{1,0:T(8,128)S(1)} %get-tuple-element.56), channel_id=1, source_target_pairs={{1,2},{2,1},{3,4},{4,3},{5,6},{6,5},{7,8},{8,7},{9,10},{10,9},{11,... | collective-permute-start | bytes 294920 | tf_op jit(solution)/shard_map/ppermute | solution.py:27
  41.9 6.6 %collective-permute-start.10 = (f32[192,128]{1,0:T(8,128)S(1)}, f32[192,128]{1,0:T(8,128)S(1)}, u32[]{:S(2)}, u32[]{:S(2)}) collective-permute-start(f32[192,128]{1,0:T(8,128)S(1)} %get-tuple-element.57), channel_id=1, source_target_pairs={{32,64},{64,32},{96,128},{128,96},{160,192},{192,160},{224,0},{0,2... | collective-permute-start | bytes 294920 | tf_op jit(solution)/shard_map/ppermute | solution.py:27
  43.7 4.9 %collective-permute-start.11 = (f32[192,128]{1,0:T(8,128)S(1)}, f32[192,128]{1,0:T(8,128)S(1)}, u32[]{:S(2)}, u32[]{:S(2)}) collective-permute-start(f32[192,128]{1,0:T(8,128)S(1)} %get-tuple-element.58), channel_id=1, source_target_pairs={{0,32},{32,0},{64,96},{96,64},{128,160},{160,128},{192,224},{224,1... | collective-permute-start | bytes 294920 | tf_op jit(solution)/shard_map/ppermute | solution.py:27

commit v3 on v2

--- a/solution.py
+++ b/solution.py
@@ -29,7 +29,7 @@
 
 STEPS = (("cross", 1), ("grav", 0), ("grav", 1), ("cross", 0))
 CHIP_FIRST = (3, 0, 2, 1)
-CHIP_LAST = (0, 2, 1, 3)
+CHIP_THIRD = (0, 2, 3, 1)
 
 
 def exchange(sent, order):
@@ -246,8 +246,8 @@
     fibres = table.shape[0] - hot_near.shape[1] - LANES
     quarter = width // 4
     parts = (part0, part1, part2, part3)
-    blocks = incoming([part[:width, :] for part in parts], CHIP_LAST)
-    packed = incoming([part[width:, :] for part in parts], CHIP_LAST)
+    blocks = incoming([part[:width, :] for part in parts], CHIP_THIRD)
+    packed = incoming([part[width:, :] for part in parts], CHIP_THIRD)
     group = lane_group(quarter)
     arrived = []
     for q in range(4):
@@ -269,7 +269,7 @@
 def sweep_kernel(part0, part1, part2, part3, partial, table, stacked, kind,
                  hot_near, near_state, near_in, rate, near_lam, out0, out1, out2, out3, extra):
     parts = [part[...] for part in (part0, part1, part2, part3)]
-    for i, block in enumerate(incoming(parts, CHIP_LAST)):
+    for i, block in enumerate(incoming(parts, CHIP_THIRD)):
         extra[:, i * LANES:(i + 1) * LANES] = split(block, 3)
     fibres = table.shape[0] - LANES - extra.shape[1]
     rate_body(partial, extra, table, fibres, stacked, kind, rate)
@@ -351,7 +351,7 @@
     *sent, near_velocity = call(
         send_kernel, [((width + width // 4, LANES), F32)] * 4 + [near_shape], held, flops=2 << 30, space=pltpu.HBM,
         scratch=[pltpu.VMEM(x.shape, x.dtype) for x in held] + [pltpu.SemaphoreType.DMA((len(held),)), pltpu.VMEM((fibres, near), BF16), pltpu.VMEM((fibres, LANES), BF16)])
-    halo = exchange(sent, CHIP_LAST)
+    halo = exchange(sent, CHIP_THIRD)
     table, hot_near, hot_land, kind, partial, lam, near_state, stacked = call(
         setup_kernel,
         [((total, count), BF16), ((count, near), BF16), ((LANES, fibres), BF16),
@@ -364,7 +364,7 @@
         (*halo, partial, table, stacked, kind, hot_near, near_state),
         scratch=[pltpu.VMEM((3 * width, near + LANES), BF16)], flops=4 << 30)
     for repeat in range(1, SWEEPS):
-        halo = exchange(sent, CHIP_LAST if repeat < SWEEPS - 1 else CHIP_FIRST)
+        halo = exchange(sent, CHIP_THIRD if repeat < SWEEPS - 1 else CHIP_FIRST)
         if repeat == 1:
             lam, partial, hot_first = call(
                 own_first_kernel, [big, partial_shape, ((count, fibres), BF16)],

time: 54.1 us -> 54.6 us (level)
  starting transfers between devices: 21.2 us -> 22.4 us
  waiting for transfers between devices: 0.85 us -> 0.08 us
    ppermute x12, starting transfers between devices: 21.2 us -> 22.4 us  [swap(): return lax.ppermute(x, axis, pairs)]
    ppermute x12, waiting for transfers between devices: 0.85 us -> 0.08 us  [swap(): return lax.ppermute(x, axis, pairs)]
  transfers between devices with their start and end apart: 12 -> 12, of which waited for: 2 -> 1; matrix products, arithmetic and copies ran while one was open for 0% -> 0% of each run, Pallas kernels for 26% -> 26%
where the time goes in v3:
time: 54.6 us; the launch traced here: 54.5 us
  Pallas kernels  30.2 us (55%)
  starting transfers between devices  22.4 us (41%)
  between operations  1.72 us (3%)
    pallas_call x7, Pallas kernels, call(): pl.pallas_call(kernel, out_shape=[jax.ShapeDtypeStruct(s, d) for s, d in...  30.2 us
    ppermute x12, starting transfers between devices, swap(): return lax.ppermute(x, axis, pairs)  22.4 us
  transfers between devices with their start and end apart: 12, of which 1 were waited for; matrix products, arithmetic and copies ran while one was open for 0% of the time, Pallas kernels for 26%

profile of v3, /device:TPU:8, one launch (start us, length us, event | category | flops | bytes accessed | tf_op | source)
XLA Modules:
  0.0 54.5 jit_solution(17836672571246229591)
XLA Ops:
  0.7 2.6 %shard_map.104 = (f32[240,128]{1,0:T(8,128)S(1)}, f32[240,128]{1,0:T(8,128)S(1)}, f32[240,128]{1,0:T(8,128)S(1)}, f32[240,128]{1,0:T(8,128)S(1)}, f32[192,512]{1,0:T(8,128)S(1)}) custom-call(f32[192,1024]{1,0:T(8,128)} %bitcast.7, f32[192,1024]{1,0:T(8,128)} %bitcast.5, s32[4,128]{1,0:T(4,128)} %near.1, s32[4,32]{1,0:T(4,128)} %send.1), custom_call_target="tpu_custom_call" | custom-call | flops 2147483648 | bytes 4194304 | tf_op jit(solution)/shard_map/pallas_call | solution.py:326
  3.3 8.0 %collective-permute-start = (f32[240,128]{1,0:T(8,128)S(1)}, f32[240,128]{1,0:T(8,128)S(1)}, u32[]{:S(2)}, u32[]{:S(2)}) collective-permute-start(f32[240,128]{1,0:T(8,128)S(1)} %get-tuple-element.34), channel_id=1, source_target_pairs={{1,2},{2,1},{3,4},{4,3},{5,6},{6,5},{7,8},{8,7},{9,10},{10,9},{11,... | collective-permute-start | bytes 368648 | tf_op jit(solution)/shard_map/ppermute | solution.py:27
  11.3 0.9 %collective-permute-start.1 = (f32[240,128]{1,0:T(8,128)S(1)}, f32[240,128]{1,0:T(8,128)S(1)}, u32[]{:S(2)}, u32[]{:S(2)}) collective-permute-start(f32[240,128]{1,0:T(8,128)S(1)} %get-tuple-element.35), channel_id=1, source_target_pairs={{32,64},{64,32},{96,128},{128,96},{160,192},{192,160},{224,0},{0,2... | collective-permute-start | bytes 368648 | tf_op jit(solution)/shard_map/ppermute | solution.py:27
  12.2 0.0 collective-permute-start.2
  12.2 2.1 %collective-permute-start.3 = (f32[240,128]{1,0:T(8,128)S(1)}, f32[240,128]{1,0:T(8,128)S(1)}, u32[]{:S(2)}, u32[]{:S(2)}) collective-permute-start(f32[240,128]{1,0:T(8,128)S(1)} %get-tuple-element.37), channel_id=1, source_target_pairs={{0,32},{32,0},{64,96},{96,64},{128,160},{160,128},{192,224},{224,1... | collective-permute-start | bytes 368648 | tf_op jit(solution)/shard_map/ppermute | solution.py:27
  15.1 4.7 %shard_map.105 = (bf16[1664,2048]{1,0:T(8,128)(2,1)S(1)}, bf16[2048,512]{1,0:T(8,128)(2,1)S(1)}, bf16[128,1024]{1,0:T(8,128)(2,1)S(1)}, s32[1,2048]{1,0:T(1,128)...) custom-call(s32[1]{0:T(128)S(6)} %copy.11.live, ...), custom_call_target="tpu_custom_call" | custom-call | flops 8589934592 | bytes 4194304 | tf_op jit(solution)/shard_map/pallas_call | solution.py:326
  19.8 0.0 collective-permute-done.part0
  19.8 0.0 collective-permute-done.1.part1
  19.8 0.0 collective-permute-done.3.part3
  19.9 4.1 %shard_map.106 = (bf16[384,2048]{1,0:T(8,128)(2,1)S(1)}, f32[192,512]{1,0:T(8,128)S(1)}, f32[192,128]{1,0:T(8,128)S(1)}, f32[192,128]{1,0:T(8,128)S(1)}, f32[192...) custom-call(f32[240,128]{1,0:T(8,128)S(1)} %collective-permute-done.part0, ...), custom_call_target="tpu_custom_call" | custom-call | flops 4294967296 | bytes 4194304 | tf_op jit(solution)/shard_map/pallas_call | solution.py:326
  24.0 1.5 %collective-permute-start.4 = (f32[192,128]{1,0:T(8,128)S(1)}, f32[192,128]{1,0:T(8,128)S(1)}, u32[]{:S(2)}, u32[]{:S(2)}) collective-permute-start(f32[192,128]{1,0:T(8,128)S(1)} %get-tuple-element.45), channel_id=1, source_target_pairs={{1,2},{2,1},{3,4},{4,3},{5,6},{6,5},{7,8},{8,7},{9,10},{10,9},{11,... | collective-permute-start | bytes 294920 | tf_op jit(solution)/shard_map/ppermute | solution.py:27
  25.5 1.6 %collective-permute-start.5 = (f32[192,128]{1,0:T(8,128)S(1)}, f32[192,128]{1,0:T(8,128)S(1)}, u32[]{:S(2)}, u32[]{:S(2)}) collective-permute-start(f32[192,128]{1,0:T(8,128)S(1)} %get-tuple-element.46), channel_id=1, source_target_pairs={{32,64},{64,32},{96,128},{128,96},{160,192},{192,160},{224,0},{0,2... | collective-permute-start | bytes 294920 | tf_op jit(solution)/shard_map/ppermute | solution.py:27
  27.1 0.0 collective-permute-start.6
  27.1 1.5 %collective-permute-start.7 = (f32[192,128]{1,0:T(8,128)S(1)}, f32[192,128]{1,0:T(8,128)S(1)}, u32[]{:S(2)}, u32[]{:S(2)}) collective-permute-start(f32[192,128]{1,0:T(8,128)S(1)} %get-tuple-element.48), channel_id=1, source_target_pairs={{0,32},{32,0},{64,96},{96,64},{128,160},{160,128},{192,224},{224,1... | collective-permute-start | bytes 294920 | tf_op jit(solution)/shard_map/ppermute | solution.py:27
  28.5 4.8 %shard_map.107 = (f32[192,1024]{1,0:T(8,128)S(1)}, f32[192,2048]{1,0:T(8,128)S(1)}, bf16[2048,1024]{1,0:T(8,128)(2,1)S(1)}) custom-call(bf16[384,2048]{1,0:T(8,128)(2,1)S(1)} %get-tuple-element.49.rate, s32[3,2048]{1,0:T(4,128)S(1)} %copy-done.4, f32[192,128]{1,0:T(8,128)S(1)} %get-tuple-element.50.landed, bf16[128,1024]{1,0:T(8,128)(2,1)S(1)} %get-tuple-element.51.hot_land, ...), custom_call_target="tpu_custom_call" | custom-call | flops 8589934592 | bytes 4194304 | tf_op jit(solution)/shard_map/pallas_call | solution.py:326
  33.4 0.0 collective-permute-done.4.part0
  33.4 4.3 %shard_map.108 = (bf16[384,2048]{1,0:T(8,128)(2,1)S(1)}, f32[192,512]{1,0:T(8,128)}, f32[192,128]{1,0:T(8,128)S(1)}, f32[192,128]{1,0:T(8,128)S(1)}, f32[192,128]{1,0:T(8,128)S(1)}, /*index=5*/f32[192,128]{1,0:T(8,128)S(1)}) custom-call(f32[192,128]{1,0:T(8,128)S(1)} %collective-permute-done.4.part0, f32[192,128]{1,0:T(8,128)S(1)} %collective-permute-done.5.part1, ...), custom_call_target="tpu_custom_call" | custom-call | flops 4294967296 | bytes 4194304 | tf_op jit(solution)/shard_map/pallas_call | solution.py:326
  37.7 0.2 collective-permute-start.8
  37.9 4.2 %collective-permute-start.9 = (f32[192,128]{1,0:T(8,128)S(1)}, f32[192,128]{1,0:T(8,128)S(1)}, u32[]{:S(2)}, u32[]{:S(2)}) collective-permute-start(f32[192,128]{1,0:T(8,128)S(1)} %get-tuple-element.56), channel_id=1, source_target_pairs={{1,2},{2,1},{3,4},{4,3},{5,6},{6,5},{7,8},{8,7},{9,10},{10,9},{11,... | collective-permute-start | bytes 294920 | tf_op jit(solution)/shard_map/ppermute | solution.py:27
  42.2 2.3 %collective-permute-start.10 = (f32[192,128]{1,0:T(8,128)S(1)}, f32[192,128]{1,0:T(8,128)S(1)}, u32[]{:S(2)}, u32[]{:S(2)}) collective-permute-start(f32[192,128]{1,0:T(8,128)S(1)} %get-tuple-element.57), channel_id=1, source_target_pairs={{32,64},{64,32},{96,128},{128,96},{160,192},{192,160},{224,0},{0,2... | collective-permute-start | bytes 294920 | tf_op jit(solution)/shard_map/ppermute | solution.py:27
  44.4 0.1 collective-permute-start.11
  44.5 4.4 %shard_map.109 = (f32[192,1024]{1,0:T(8,128)S(1)}, f32[192,2048]{1,0:T(8,128)S(1)}) custom-call(bf16[384,2048]{1,0:T(8,128)(2,1)S(1)} %get-tuple-element.59.rate, bf16[2048,1024]{1,0:T(8,128)(2,1)S(1)} %get-tuple-element.60.hot_first, f32[192,1024]{1,0:T(8,128)S(1)} %get-tuple-element.61.lam_in, f32[192,1024]{1,0:T(8,128)S(1)} %bitcast.13, ...), custom_call_target="tpu_custom_call" | custom-call | flops 8589934592 | bytes 4194304 | tf_op jit(solution)/shard_map/pallas_call | solution.py:326
  49.0 0.1 collective-permute-done.11.part3
  49.0 5.3 %shard_map.110 = (f32[192,1024]{1,0:T(8,128)}, f32[192,1024]{1,0:T(8,128)}) custom-call(f32[192,128]{1,0:T(8,128)S(1)} %collective-permute-done.8.part0, f32[192,128]{1,0:T(8,128)S(1)} %collective-permute-done.9.part1, f32[192,128]{1,0:T(8,128)S(1)} %collective-permute-done.10.part2, f32[192,128]{1,0:T(8,128)S(1)} %collective-permute-done.11.part3, ...), custom_call_target="tpu_custom_call" | custom-call | flops 4294967296 | bytes 4194304 | tf_op jit(solution)/shard_map/pallas_call | solution.py:326
  (23 shorter events, 0.1 us)
Async XLA Ops:
  0.6 14.4 %copy-start = (f32[3,64,1024]{2,1,0:T(8,128)S(1)}, f32[3,64,1024]{2,1,0:T(8,128)}, u32[]{:S(2)}) copy-start(f32[3,64,1024]{2,1,0:T(8,128)} %param.10) | copy-start | bytes 2359300
  0.6 14.4 %copy-start.1 = (bf16[8,192,192]{2,1,0:T(8,128)(2,1)S(1)}, bf16[8,192,192]{2,1,0:T(8,128)(2,1)}, u32[]{:S(2)}) copy-start(bf16[8,192,192]{2,1,0:T(8,128)(2,1)} %mobility.1) | copy-start | bytes 1769476
  0.7 14.4 %copy-start.2 = (f32[3,64,1024]{2,1,0:T(8,128)S(1)}, f32[3,64,1024]{2,1,0:T(8,128)}, u32[]{:S(2)}) copy-start(f32[3,64,1024]{2,1,0:T(8,128)} %param.9) | copy-start | bytes 2359300
  0.7 14.4 %copy-start.3 = (f32[3,64,1024]{2,1,0:T(8,128)S(1)}, f32[3,64,1024]{2,1,0:T(8,128)}, u32[]{:S(2)}) copy-start(f32[3,64,1024]{2,1,0:T(8,128)} %param.11) | copy-start | bytes 2359300
  0.7 14.4 %copy-start.4 = (s32[3,2048]{1,0:T(4,128)S(1)}, s32[3,2048]{1,0:T(4,128)}, u32[]{:S(2)}) copy-start(s32[3,2048]{1,0:T(4,128)} %contacts.3) | copy-start | bytes 73732
  0.7 14.4 %copy-start.5 = (s32[4,128]{1,0:T(4,128)S(1)}, s32[4,128]{1,0:T(4,128)}, u32[]{:S(2)}) copy-start(s32[4,128]{1,0:T(4,128)} %near.1) | copy-start | bytes 6148
  0.7 14.4 %copy-start.6 = (s32[4,32]{1,0:T(4,128)S(1)}, s32[4,32]{1,0:T(4,128)}, u32[]{:S(2)}) copy-start(s32[4,32]{1,0:T(4,128)} %send.1) | copy-start | bytes 1540
  0.7 14.4 %copy-start.7 = (s32[4,32]{1,0:T(4,128)S(1)}, s32[4,32]{1,0:T(4,128)}, u32[]{:S(2)}) copy-start(s32[4,32]{1,0:T(4,128)} %land.1) | copy-start | bytes 1540
  3.3 16.5 %collective-permute-start = (f32[240,128]{1,0:T(8,128)S(1)}, f32[240,128]{1,0:T(8,128)S(1)}, u32[]{:S(2)}, u32[]{:S(2)}) collective-permute-start(f32[240,128]{1,0:T(8,128)S(1)} %get-tuple-element.34), channel_id=1, source_target_pairs={{1,2},{2,1},{3,4},{4,3},{5,6},{6,5},{7,8},{8,7},{9,10},{10,9},{11,... | collective-permute-start | bytes 368648 | tf_op jit(solution)/shard_map/ppermute | solution.py:27
  11.3 8.5 %collective-permute-start.1 = (f32[240,128]{1,0:T(8,128)S(1)}, f32[240,128]{1,0:T(8,128)S(1)}, u32[]{:S(2)}, u32[]{:S(2)}) collective-permute-start(f32[240,128]{1,0:T(8,128)S(1)} %get-tuple-element.35), channel_id=1, source_target_pairs={{32,64},{64,32},{96,128},{128,96},{160,192},{192,160},{224,0},{0,2... | collective-permute-start | bytes 368648 | tf_op jit(solution)/shard_map/ppermute | solution.py:27
  12.2 7.6 %collective-permute-start.2 = (f32[240,128]{1,0:T(8,128)S(1)}, f32[240,128]{1,0:T(8,128)S(1)}, u32[]{:S(2)}, u32[]{:S(2)}) collective-permute-start(f32[240,128]{1,0:T(8,128)S(1)} %get-tuple-element.36), channel_id=1, source_target_pairs={{0,1},{1,0},{2,3},{3,2},{4,5},{5,4},{6,7},{7,6},{8,9},{9,8},{10,11... | collective-permute-start | bytes 368648 | tf_op jit(solution)/shard_map/ppermute | solution.py:27
  12.2 7.6 %collective-permute-start.3 = (f32[240,128]{1,0:T(8,128)S(1)}, f32[240,128]{1,0:T(8,128)S(1)}, u32[]{:S(2)}, u32[]{:S(2)}) collective-permute-start(f32[240,128]{1,0:T(8,128)S(1)} %get-tuple-element.37), channel_id=1, source_target_pairs={{0,32},{32,0},{64,96},{96,64},{128,160},{160,128},{192,224},{224,1... | collective-permute-start | bytes 368648 | tf_op jit(solution)/shard_map/ppermute | solution.py:27
  24.0 9.4 %collective-permute-start.4 = (f32[192,128]{1,0:T(8,128)S(1)}, f32[192,128]{1,0:T(8,128)S(1)}, u32[]{:S(2)}, u32[]{:S(2)}) collective-permute-start(f32[192,128]{1,0:T(8,128)S(1)} %get-tuple-element.45), channel_id=1, source_target_pairs={{1,2},{2,1},{3,4},{4,3},{5,6},{6,5},{7,8},{8,7},{9,10},{10,9},{11,... | collective-permute-start | bytes 294920 | tf_op jit(solution)/shard_map/ppermute | solution.py:27
  25.5 7.9 %collective-permute-start.5 = (f32[192,128]{1,0:T(8,128)S(1)}, f32[192,128]{1,0:T(8,128)S(1)}, u32[]{:S(2)}, u32[]{:S(2)}) collective-permute-start(f32[192,128]{1,0:T(8,128)S(1)} %get-tuple-element.46), channel_id=1, source_target_pairs={{32,64},{64,32},{96,128},{128,96},{160,192},{192,160},{224,0},{0,2... | collective-permute-start | bytes 294920 | tf_op jit(solution)/shard_map/ppermute | solution.py:27
  27.1 6.3 %collective-permute-start.6 = (f32[192,128]{1,0:T(8,128)S(1)}, f32[192,128]{1,0:T(8,128)S(1)}, u32[]{:S(2)}, u32[]{:S(2)}) collective-permute-start(f32[192,128]{1,0:T(8,128)S(1)} %get-tuple-element.47), channel_id=1, source_target_pairs={{0,1},{1,0},{2,3},{3,2},{4,5},{5,4},{6,7},{7,6},{8,9},{9,8},{10,11... | collective-permute-start | bytes 294920 | tf_op jit(solution)/shard_map/ppermute | solution.py:27
  27.1 6.3 %collective-permute-start.7 = (f32[192,128]{1,0:T(8,128)S(1)}, f32[192,128]{1,0:T(8,128)S(1)}, u32[]{:S(2)}, u32[]{:S(2)}) collective-permute-start(f32[192,128]{1,0:T(8,128)S(1)} %get-tuple-element.48), channel_id=1, source_target_pairs={{0,32},{32,0},{64,96},{96,64},{128,160},{160,128},{192,224},{224,1... | collective-permute-start | bytes 294920 | tf_op jit(solution)/shard_map/ppermute | solution.py:27
  37.7 11.3 %collective-permute-start.8 = (f32[192,128]{1,0:T(8,128)S(1)}, f32[192,128]{1,0:T(8,128)S(1)}, u32[]{:S(2)}, u32[]{:S(2)}) collective-permute-start(f32[192,128]{1,0:T(8,128)S(1)} %get-tuple-element.55), channel_id=1, source_target_pairs={{0,1},{1,0},{2,3},{3,2},{4,5},{5,4},{6,7},{7,6},{8,9},{9,8},{10,11... | collective-permute-start | bytes 294920 | tf_op jit(solution)/shard_map/ppermute | solution.py:27
  37.9 11.0 %collective-permute-start.9 = (f32[192,128]{1,0:T(8,128)S(1)}, f32[192,128]{1,0:T(8,128)S(1)}, u32[]{:S(2)}, u32[]{:S(2)}) collective-permute-start(f32[192,128]{1,0:T(8,128)S(1)} %get-tuple-element.56), channel_id=1, source_target_pairs={{1,2},{2,1},{3,4},{4,3},{5,6},{6,5},{7,8},{8,7},{9,10},{10,9},{11,... | collective-permute-start | bytes 294920 | tf_op jit(solution)/shard_map/ppermute | solution.py:27
  42.2 6.8 %collective-permute-start.10 = (f32[192,128]{1,0:T(8,128)S(1)}, f32[192,128]{1,0:T(8,128)S(1)}, u32[]{:S(2)}, u32[]{:S(2)}) collective-permute-start(f32[192,128]{1,0:T(8,128)S(1)} %get-tuple-element.57), channel_id=1, source_target_pairs={{32,64},{64,32},{96,128},{128,96},{160,192},{192,160},{224,0},{0,2... | collective-permute-start | bytes 294920 | tf_op jit(solution)/shard_map/ppermute | solution.py:27
  44.4 4.6 %collective-permute-start.11 = (f32[192,128]{1,0:T(8,128)S(1)}, f32[192,128]{1,0:T(8,128)S(1)}, u32[]{:S(2)}, u32[]{:S(2)}) collective-permute-start(f32[192,128]{1,0:T(8,128)S(1)} %get-tuple-element.58), channel_id=1, source_target_pairs={{0,32},{32,0},{64,96},{96,64},{128,160},{160,128},{192,224},{224,1... | collective-permute-start | bytes 294920 | tf_op jit(solution)/shard_map/ppermute | solution.py:27
